TPU v7x, 32 devices: a whole 2x2x4 slice. The times are simulated.
32 devices in a mesh: seq: 8 (over y, x, core), head: 4 (over z).
Axes of the slice: x: 2, y: 2, z: 4, core: 2. Of those that a mesh axis runs over, the one named last changes fastest.
Arguments:
- inputs: bfloat16 [4, 4096, 1024], P(None, 'seq'), may hold values from -6 to 6
- lengths: int32 [4], replicated, may hold values from 1024 to 4096, as said below
- decays: float32 [2, 4, 8, 8], P(None, None, 'seq'), may hold values from 0 to 1
- norm_gain: float32 [1024], replicated, may hold values from 0.5 to 1.5
- query_proj: bfloat16 [1024, 1024], P(None, 'head'), may hold values from -0.1875 to 0.1875
- key_proj: bfloat16 [1024, 1024], P(None, 'head'), may hold values from -0.1875 to 0.1875
- value_proj: bfloat16 [1024, 1024], P(None, 'head'), may hold values from -0.1875 to 0.1875
- gate_proj: bfloat16 [1024, 1024], P(None, 'head'), may hold values from -0.1875 to 0.1875
- conv_taps: bfloat16 [3, 4, 1024], P(None, None, 'head'), may hold values from -3 to 3
- pers_keys: bfloat16 [16, 1024], P(None, 'head'), may hold values from -6 to 6
- pers_values: bfloat16 [16, 1024], P(None, 'head'), may hold values from -6 to 6
- out_proj: bfloat16 [1024, 1024], P('head'), may hold values from -0.375 to 0.375
- ffn_gain: float32 [1024], replicated, may hold values from 0.5 to 1.5
- ffn_gate: bfloat16 [1024, 2816], P(None, 'head'), may hold values from -0.1875 to 0.1875
- ffn_up: bfloat16 [1024, 2816], P(None, 'head'), may hold values from -0.1875 to 0.1875
- ffn_down: bfloat16 [2816, 1024], P('head'), may hold values from -0.15625 to 0.15625
- cotangent: bfloat16 [4, 4096, 1024], P(None, 'seq'), may hold values from -6 to 6
Outputs:
- output: bfloat16 [4, 4096, 1024], P(None, 'seq')
- input_grad: bfloat16 [4, 4096, 1024], P(None, 'seq')
- grad_norm_gain: float32 [1024], replicated
- grad_query: float32 [1024, 1024], P('seq', 'head')
- grad_key: float32 [1024, 1024], P('seq', 'head')
- grad_value: float32 [1024, 1024], P('seq', 'head')
- grad_gate: float32 [1024, 1024], P('seq', 'head')
- grad_conv: float32 [3, 4, 1024], P(None, None, 'head')
- grad_pers_keys: float32 [16, 1024], P(None, 'head')
- grad_pers_values: float32 [16, 1024], P(None, 'head')
- grad_out_proj: float32 [1024, 1024], P('head', 'seq')
- grad_ffn_gain: float32 [1024], replicated
- grad_ffn_gate: float32 [1024, 2816], P('seq', 'head')
- grad_ffn_up: float32 [1024, 2816], P('seq', 'head')
- grad_ffn_down: float32 [2816, 1024], P('head', 'seq')
Inputs may be any that keep to these rules, and one draw needn't show every extreme that they name: `lengths`: one sequence, chosen by the seed, is 4096 long.
All inputs are finite; a program needn't handle non-finite values.
Results may differ from a plain program's by a relative error of at most 0.02.
Values may be sent and summed in bfloat16 or wider, within the bound.
A program may use at most 320 MiB of HBM per device.

v0:
```python
import jax
import jax.numpy as jnp
from jax import lax
from jax.sharding import PartitionSpec as P

DH = 128
P_SIZE = 16
KW = 4


EPSILON = 1e-06


def from_behind(value, axis, steps):
    count = lax.axis_size(axis)
    initial, last = (max(0, -steps), min(count, count - steps))
    return lax.ppermute(value, axis, [(source, source + steps) for source in range(initial, last)])


def carried_in(part, axis, combine, identity, reverse):
    count = lax.axis_size(axis)
    place = lax.axis_index(axis)
    ahead = count - 1 - place if reverse else place
    gathered = jax.tree.map(lambda a: lax.all_gather(a, axis), part)
    state = jax.tree.map(lambda a, e: jnp.zeros_like(a) + jnp.asarray(e, a.dtype), part, identity)

    def one(hop, state):
        source = count - 1 - hop if reverse else hop
        return combine(
            state, jax.tree.map(lambda a: lax.dynamic_index_in_dim(a, source, 0, False), gathered)
        )

    return lax.fori_loop(0, ahead, one, state)


def norm_keep(values):
    inverse = lax.rsqrt(jnp.mean(values * values, axis=-1, keepdims=True) + EPSILON)
    return (values * inverse, inverse)


def norm_back(grad, normed, inverse):
    return inverse * (grad - normed * jnp.mean(grad * normed, axis=-1, keepdims=True))


def silu_slope(values):
    sigma = jax.nn.sigmoid(values)
    return sigma * (1.0 + values * (1.0 - sigma))


def widen(coeff):
    return coeff[..., None, None]


def combine_forward(early, later):
    a_one, b_one, e_one, m_one, s_one = early
    a_two, b_two, e_two, m_two, s_two = later
    return (
        a_two * a_one,
        a_two * b_one + b_two * e_one,
        e_two * e_one,
        widen(a_two) * m_one + widen(b_two) * s_one + m_two,
        widen(e_two) * s_one + s_two,
    )


def combine_backward(early, later):
    a_one, b_one, e_one, m_one, s_one = early
    a_two, b_two, e_two, m_two, s_two = later
    return (
        a_two * a_one,
        b_two * a_one + e_two * b_one,
        e_two * e_one,
        widen(a_two) * m_one + m_two,
        widen(b_two) * m_one + widen(e_two) * s_one + s_two,
    )


def local(
    inputs,
    lengths,
    decays,
    norm_gain,
    query_proj,
    key_proj,
    value_proj,
    gate_proj,
    conv_taps,
    pers_keys,
    pers_values,
    out_proj,
    ffn_gain,
    ffn_gate,
    ffn_up,
    ffn_down,
    cotangent,
):
    seq_count, seg_len, features = inputs.shape
    local_width = query_proj.shape[1]
    head_count = local_width // DH
    decays = lax.dynamic_slice_in_dim(decays, lax.axis_index("head") * head_count, head_count, 3)
    rim = KW - 1
    offset = lax.axis_index("seq") * seg_len
    positions = offset + jnp.arange(seg_len, dtype=jnp.int32)
    live = (positions[None, :] < lengths[:, None]).astype(jnp.float32)
    live_three = live[:, :, None]
    alpha = decays[0, :, 0, :]
    eta = decays[1, :, 0, :]

    def by_head(values):
        return values.reshape(values.shape[:-1] + (head_count, DH))

    x_float = inputs.astype(jnp.float32)
    n_one, inv_one = norm_keep(x_float)
    flat_one = (n_one * norm_gain).astype(jnp.bfloat16).reshape(-1, features)

    def project(matrix):
        return jnp.dot(flat_one, matrix, preferred_element_type=jnp.float32).reshape(
            seq_count, seg_len, -1
        )

    projected = jnp.stack([project(query_proj), project(key_proj), project(value_proj)]).astype(
        jnp.bfloat16
    )
    gate_pre = project(gate_proj)
    tails = projected[:, :, seg_len - rim :, :]
    before = from_behind(tails, "seq", 1)
    padded = jnp.concatenate([before, projected], axis=2).astype(jnp.float32)
    taps = conv_taps.astype(jnp.float32)
    conv_sum = taps[:, 0][:, None, None, :] * padded[:, :, rim : rim + seg_len]
    for lag in range(1, KW):
        conv_sum = (
            conv_sum
            + taps[:, lag][:, None, None, :] * padded[:, :, rim - lag : rim - lag + seg_len]
        )
    acts = jax.nn.silu(conv_sum)
    q_normed, q_inverse = norm_keep(by_head(acts[0]))
    k_normed, k_inverse = norm_keep(by_head(acts[1]))
    query = q_normed.astype(jnp.bfloat16)
    keyed = k_normed.astype(jnp.bfloat16)
    valued = by_head(acts[2]).astype(jnp.bfloat16)
    live_four = live[:, :, None, None]
    masked_value = valued * live_four.astype(jnp.bfloat16)
    write = (
        jnp.einsum("stha,sthb->shab", masked_value, keyed, preferred_element_type=jnp.float32)
        / seg_len
    )
    ones_coeff = jnp.ones_like(alpha)
    zero_coeff = jnp.zeros_like(alpha)
    zero_state = jnp.zeros_like(write)
    identity = (ones_coeff, zero_coeff, ones_coeff, zero_state, zero_state)
    prefix = carried_in((alpha, eta, eta, write, write), "seq", combine_forward, identity, False)
    memory = prefix[3].astype(jnp.bfloat16)
    raw_read = jnp.einsum("shab,sthb->stha", memory, query, preferred_element_type=jnp.float32)
    readout, read_inverse = norm_keep(raw_read)
    pers_k = jnp.broadcast_to(
        pers_keys.reshape(1, P_SIZE, head_count, DH), (seq_count, P_SIZE, head_count, DH)
    )
    pers_v = jnp.broadcast_to(
        pers_values.reshape(1, P_SIZE, head_count, DH), (seq_count, P_SIZE, head_count, DH)
    )
    keys_all = jnp.concatenate([pers_k, keyed], axis=1)
    values_all = jnp.concatenate([pers_v, valued], axis=1)
    key_valid = jnp.concatenate([jnp.ones((seq_count, P_SIZE), jnp.float32), live], axis=1)
    rows_index = jnp.arange(seg_len)[:, None]
    column = jnp.arange(P_SIZE + seg_len)[None, :] - P_SIZE
    allowed = (column < 0)[None] | (column <= rows_index)[None] & (key_valid[:, None, :] > 0.5)
    scale = DH ** (-0.5)

    def scores_of():
        raw = (
            jnp.einsum("sthd,suhd->shtu", query, keys_all, preferred_element_type=jnp.float32)
            * scale
        )
        return jnp.where(allowed[:, None], raw, -1e30)

    score = scores_of()
    top_score = jnp.max(score, axis=-1, keepdims=True)
    log_total = top_score + jnp.log(jnp.sum(jnp.exp(score - top_score), axis=-1, keepdims=True))
    prob_low = jnp.exp(score - log_total).astype(jnp.bfloat16)
    attended = jnp.einsum(
        "shtu,suhd->sthd", prob_low, values_all, preferred_element_type=jnp.float32
    )
    sigma_gate = jax.nn.sigmoid(gate_pre)
    readout_flat = readout.reshape(seq_count, seg_len, local_width)
    mixed = (attended.reshape(seq_count, seg_len, local_width) + sigma_gate * readout_flat).astype(
        jnp.bfloat16
    )
    mixed_flat = mixed.reshape(-1, local_width)
    attn_part = jnp.dot(mixed_flat, out_proj, preferred_element_type=jnp.float32)
    attn_share = lax.psum_scatter(attn_part, "head", scatter_dimension=0, tiled=True)
    attn_part = lax.all_gather(attn_share, "head", axis=0, tiled=True)
    attn_out = attn_part.reshape(seq_count, seg_len, features)
    middle = x_float + live_three * attn_out
    n_two, inv_two = norm_keep(middle)
    flat_two = (n_two * ffn_gain).astype(jnp.bfloat16).reshape(-1, features)
    gate_value = jnp.dot(flat_two, ffn_gate, preferred_element_type=jnp.float32)
    up_value = jnp.dot(flat_two, ffn_up, preferred_element_type=jnp.float32)
    silu_gate = jax.nn.silu(gate_value)
    hidden = (silu_gate * up_value).astype(jnp.bfloat16)
    ffn_part = jnp.dot(hidden, ffn_down, preferred_element_type=jnp.float32).reshape(
        seq_count, seg_len, features
    )
    shares = lax.psum_scatter(
        ffn_part.astype(jnp.bfloat16), "head", scatter_dimension=2, tiled=True
    ).astype(jnp.float32)
    share_width = shares.shape[2]
    middle_share = lax.dynamic_slice_in_dim(
        middle, lax.axis_index("head") * share_width, share_width, 2
    )
    output = lax.all_gather(
        (middle_share + live_three * shares).astype(jnp.bfloat16), "head", axis=2, tiled=True
    )
    grad_float = cotangent.astype(jnp.float32)
    ffn_grad = (live_three * grad_float).astype(jnp.bfloat16).reshape(-1, features)
    grad_down = jnp.einsum("tf,td->fd", hidden, ffn_grad, preferred_element_type=jnp.float32)
    hidden_grad = jnp.einsum("td,fd->tf", ffn_grad, ffn_down, preferred_element_type=jnp.float32)
    gate_grad = (hidden_grad * up_value * silu_slope(gate_value)).astype(jnp.bfloat16)
    up_grad = (hidden_grad * silu_gate).astype(jnp.bfloat16)
    grad_ffn_gate = jnp.einsum("td,tf->df", flat_two, gate_grad, preferred_element_type=jnp.float32)
    grad_ffn_up = jnp.einsum("td,tf->df", flat_two, up_grad, preferred_element_type=jnp.float32)
    two_part = jnp.einsum(
        "tf,df->td", gate_grad, ffn_gate, preferred_element_type=jnp.float32
    ) + jnp.einsum("tf,df->td", up_grad, ffn_up, preferred_element_type=jnp.float32)
    two_share = lax.psum_scatter(two_part, "head", scatter_dimension=0, tiled=True)
    two_part = lax.all_gather(two_share, "head", axis=0, tiled=True)
    two_grad = two_part.reshape(seq_count, seg_len, features)
    grad_ffn_gain = jnp.sum(two_grad * n_two, axis=(0, 1))
    middle_grad = grad_float + norm_back(two_grad * ffn_gain, n_two, inv_two)
    attn_grad = (live_three * middle_grad).astype(jnp.bfloat16).reshape(-1, features)
    grad_out_proj = jnp.einsum(
        "tl,td->ld", mixed_flat, attn_grad, preferred_element_type=jnp.float32
    )
    mixed_grad = jnp.einsum(
        "td,ld->tl", attn_grad, out_proj, preferred_element_type=jnp.float32
    ).reshape(seq_count, seg_len, local_width)
    att_grad = by_head(mixed_grad.astype(jnp.bfloat16))
    gate_pre_grad = (mixed_grad * readout_flat * sigma_gate * (1.0 - sigma_gate)).astype(
        jnp.bfloat16
    )
    read_grad = norm_back(by_head(mixed_grad * sigma_gate), readout, read_inverse).astype(
        jnp.bfloat16
    )
    prior_grad = jnp.einsum("stha,sthb->shab", read_grad, query, preferred_element_type=jnp.float32)
    query_mem_grad = jnp.einsum(
        "shab,stha->sthb", memory, read_grad, preferred_element_type=jnp.float32
    )
    score_again = scores_of()
    prob_float = jnp.exp(score_again - log_total)
    prob_again = prob_float.astype(jnp.bfloat16)
    prob_grad = jnp.einsum(
        "sthd,suhd->shtu", att_grad, values_all, preferred_element_type=jnp.float32
    )
    row_dot = jnp.sum(prob_float * prob_grad, axis=-1, keepdims=True)
    score_grad = (prob_float * (prob_grad - row_dot)).astype(jnp.bfloat16)
    query_att_grad = (
        jnp.einsum("shtu,suhd->sthd", score_grad, keys_all, preferred_element_type=jnp.float32)
        * scale
    )
    keys_grad = (
        jnp.einsum("shtu,sthd->suhd", score_grad, query, preferred_element_type=jnp.float32) * scale
    )
    values_grad = jnp.einsum(
        "shtu,sthd->suhd", prob_again, att_grad, preferred_element_type=jnp.float32
    )
    grad_pers_keys = jnp.sum(keys_grad[:, :P_SIZE], axis=0).reshape(P_SIZE, local_width)
    grad_pers_values = jnp.sum(values_grad[:, :P_SIZE], axis=0).reshape(P_SIZE, local_width)
    suffix = carried_in(
        (alpha, eta, eta, prior_grad, zero_state), "seq", combine_backward, identity, True
    )
    write_grad = (suffix[3] + suffix[4]).astype(jnp.bfloat16)
    value_grad = (
        values_grad[:, P_SIZE:]
        + live_four
        * jnp.einsum("shab,sthb->stha", write_grad, keyed, preferred_element_type=jnp.float32)
        / seg_len
    )
    key_grad = (
        keys_grad[:, P_SIZE:]
        + jnp.einsum(
            "shab,stha->sthb", write_grad, masked_value, preferred_element_type=jnp.float32
        )
        / seg_len
    )
    query_grad = query_att_grad + query_mem_grad
    act_grad = jnp.stack(
        [
            norm_back(query_grad, q_normed, q_inverse),
            norm_back(key_grad, k_normed, k_inverse),
            value_grad,
        ]
    ).reshape(3, seq_count, seg_len, local_width)
    conv_grad = act_grad * silu_slope(conv_sum)
    padded_grad = taps[:, 0][:, None, None, :] * jnp.pad(
        conv_grad, ((0, 0), (0, 0), (rim, 0), (0, 0))
    )
    for lag in range(1, KW):
        padded_grad = padded_grad + taps[:, lag][:, None, None, :] * jnp.pad(
            conv_grad, ((0, 0), (0, 0), (rim - lag, lag), (0, 0))
        )
    grad_conv = jnp.stack(
        [
            jnp.sum(conv_grad * padded[:, :, rim - lag : rim - lag + seg_len], axis=(1, 2))
            for lag in range(KW)
        ],
        axis=1,
    )
    from_next = from_behind(padded_grad[:, :, :rim].astype(jnp.bfloat16), "seq", -1).astype(
        jnp.float32
    )
    own_grad = padded_grad[:, :, rim:]
    pre_grad = (
        jnp.concatenate(
            [own_grad[:, :, : seg_len - rim], own_grad[:, :, seg_len - rim :] + from_next], axis=2
        )
        .astype(jnp.bfloat16)
        .reshape(3, -1, local_width)
    )
    gate_flat = gate_pre_grad.reshape(-1, local_width)
    grad_query = jnp.einsum("td,tl->dl", flat_one, pre_grad[0], preferred_element_type=jnp.float32)
    grad_key = jnp.einsum("td,tl->dl", flat_one, pre_grad[1], preferred_element_type=jnp.float32)
    grad_value = jnp.einsum("td,tl->dl", flat_one, pre_grad[2], preferred_element_type=jnp.float32)
    grad_gate = jnp.einsum("td,tl->dl", flat_one, gate_flat, preferred_element_type=jnp.float32)
    one_part = (
        jnp.einsum("tl,dl->td", pre_grad[0], query_proj, preferred_element_type=jnp.float32)
        + jnp.einsum("tl,dl->td", pre_grad[1], key_proj, preferred_element_type=jnp.float32)
        + jnp.einsum("tl,dl->td", pre_grad[2], value_proj, preferred_element_type=jnp.float32)
        + jnp.einsum("tl,dl->td", gate_flat, gate_proj, preferred_element_type=jnp.float32)
    )
    one_share = lax.psum_scatter(
        one_part.astype(jnp.bfloat16), "head", scatter_dimension=0, tiled=True
    ).astype(jnp.float32)
    one_part = lax.all_gather(one_share.astype(jnp.bfloat16), "head", axis=0, tiled=True).astype(
        one_share.dtype
    )
    one_grad = one_part.reshape(seq_count, seg_len, features)
    grad_norm_gain = jnp.sum(one_grad * n_one, axis=(0, 1))
    input_grad = (middle_grad + norm_back(one_grad * norm_gain, n_one, inv_one)).astype(
        jnp.bfloat16
    )
    small_sums = lax.psum(
        (grad_norm_gain, grad_ffn_gain, grad_conv, grad_pers_keys, grad_pers_values), "seq"
    )
    sums = (
        lax.psum_scatter(
            grad_query.astype(jnp.bfloat16), "seq", scatter_dimension=0, tiled=True
        ).astype(jnp.float32),
        lax.psum_scatter(
            grad_key.astype(jnp.bfloat16), "seq", scatter_dimension=0, tiled=True
        ).astype(jnp.float32),
        lax.psum_scatter(
            grad_value.astype(jnp.bfloat16), "seq", scatter_dimension=0, tiled=True
        ).astype(jnp.float32),
        lax.psum_scatter(
            grad_gate.astype(jnp.bfloat16), "seq", scatter_dimension=0, tiled=True
        ).astype(jnp.float32),
        lax.psum_scatter(
            grad_ffn_gate.astype(jnp.bfloat16), "seq", scatter_dimension=0, tiled=True
        ).astype(jnp.float32),
        lax.psum_scatter(
            grad_ffn_up.astype(jnp.bfloat16), "seq", scatter_dimension=0, tiled=True
        ).astype(jnp.float32),
        lax.psum_scatter(
            grad_out_proj.astype(jnp.bfloat16), "seq", scatter_dimension=1, tiled=True
        ).astype(jnp.float32),
        lax.psum_scatter(
            grad_down.astype(jnp.bfloat16), "seq", scatter_dimension=1, tiled=True
        ).astype(jnp.float32),
    )
    return (
        output,
        input_grad,
        small_sums[0],
        sums[0],
        sums[1],
        sums[2],
        sums[3],
        small_sums[2],
        small_sums[3],
        small_sums[4],
        sums[6],
        small_sums[1],
        sums[4],
        sums[5],
        sums[7],
    )


def solution(mesh):
    in_specs = (
        P(None, "seq", None),
        P(),
        P(None, None, "seq", None),
        P(),
        P(None, "head"),
        P(None, "head"),
        P(None, "head"),
        P(None, "head"),
        P(None, None, "head"),
        P(None, "head"),
        P(None, "head"),
        P("head", None),
        P(),
        P(None, "head"),
        P(None, "head"),
        P("head", None),
        P(None, "seq", None),
    )
    out_specs = (
        P(None, "seq", None),
        P(None, "seq", None),
        P(),
        P("seq", "head"),
        P("seq", "head"),
        P("seq", "head"),
        P("seq", "head"),
        P(None, None, "head"),
        P(None, "head"),
        P(None, "head"),
        P("head", "seq"),
        P(),
        P("seq", "head"),
        P("seq", "head"),
        P("head", "seq"),
    )
    return jax.shard_map(local, mesh=mesh, in_specs=in_specs, out_specs=out_specs, check_vma=False)
```

profile of v0, /device:TPU:0, one launch (start us, length us, event | category | flops | bytes accessed | tf_op | source)
XLA Modules:
  0.0 1520.6 jit_solution(362630862159580063)
XLA Ops:
  45.6 13.2 all-gather
  58.9 8.4 all-gather.1
  108.9 6.4 add_convert_fusion.2
  120.9 159.8 %reduce-scatter.21.cloned.1.call-done = f32[512,1024]{1,0:T(8,128)} async-done(((f32[2048,1024]{1,0:T(8,128)}), f32[512,1024]{1,0:T(8,128)}) %reduce-scatter.21.cloned.1.call-update) | async-done | bytes 2097168 | tf_op jit(solution)/shard_map/reduce_scatter | solution.py:190
  280.9 151.7 %all-gather.11.cloned.1.call-done = f32[2048,1024]{1,0:T(8,128)} async-done(((f32[512,1024]{1,0:T(8,128)}), f32[2048,1024]{1,0:T(8,128)}) %all-gather.11.cloned.1.call-update) | async-done | bytes 8388624 | tf_op jit(solution)/shard_map/all_gather | solution.py:191
  432.7 7.1 multiply_reduce_fusion.3
  451.3 8.3 multiply_convert_fusion.3
  469.1 142.8 %reduce-scatter.25.cloned.1.call-done = f32[512,1024]{1,0:T(8,128)} async-done(((f32[2048,1024]{1,0:T(8,128)}), f32[512,1024]{1,0:T(8,128)}) %reduce-scatter.25.cloned.1.call-update) | async-done | bytes 2097168 | tf_op jit(solution)/shard_map/reduce_scatter | solution.py:224
  611.9 151.7 %all-gather.15.cloned.1.call-done = f32[2048,1024]{1,0:T(8,128)} async-done(((f32[512,1024]{1,0:T(8,128)}), f32[2048,1024]{1,0:T(8,128)}) %all-gather.15.cloned.1.call-update) | async-done | bytes 8388624 | tf_op jit(solution)/shard_map/all_gather | solution.py:225
  763.7 10.3 multiply_reduce_fusion.1
  800.5 6.9 convolution_convert_fusion
  809.0 6.9 convolution_bitcast_fusion
  835.7 14.8 while.37
  871.0 14.0 multiply_reduce_fusion.7
  904.5 9.8 add_convert_fusion
  914.4 7.4 convolution_convert_fusion.3
  924.4 7.4 convolution_convert_fusion.1
  934.8 7.3 convolution_convert_fusion.2
  974.2 20.7 %reduce-scatter.27.cloned.1.call-done = bf16[512,1024]{1,0:T(8,128)(2,1)} async-done(((bf16[2048,1024]{1,0:T(8,128)(2,1)}), bf16[512,1024]{1,0:T(8,128)(2,1)}) %reduce-scatter.27.cloned.1.call-update) | async-done | bytes 1048592 | tf_op jit(solution)/shard_map/reduce_scatter | solution.py:329
  995.0 42.3 %reduce-scatter.43.cloned.1.call-done = bf16[128,704]{1,0:T(8,128)(2,1)} async-done(((bf16[1024,704]{1,0:T(8,128)(2,1)}), bf16[128,704]{1,0:T(8,128)(2,1)}) %reduce-scatter.43.cloned.1.call-update) | async-done | bytes 180240
  1039.1 39.8 %reduce-scatter.41.cloned.1.call-done = bf16[128,704]{1,0:T(8,128)(2,1)} async-done(((bf16[1024,704]{1,0:T(8,128)(2,1)}), bf16[128,704]{1,0:T(8,128)(2,1)}) %reduce-scatter.41.cloned.1.call-update) | async-done | bytes 180240
  1080.8 39.9 %reduce-scatter.39.cloned.1.call-done = bf16[128,704]{1,0:T(8,128)(2,1)} async-done(((bf16[1024,704]{1,0:T(8,128)(2,1)}), bf16[128,704]{1,0:T(8,128)(2,1)}) %reduce-scatter.39.cloned.1.call-update) | async-done | bytes 180240
  1122.6 80.7 %all-gather.13.cloned.1.call-done = bf16[4,512,1024]{2,1,0:T(8,128)(2,1)} async-done(((bf16[4,512,256]{2,1,0:T(8,128)(2,1)}), bf16[4,512,1024]{2,1,0:T(8,128)(2,1)}) %all-gather.13.cloned.1.call-update) | async-done | bytes 4194320 | tf_op jit(solution)/shard_map/all_gather | solution.py:210
  1205.0 33.7 %reduce-scatter.37.cloned.1.call-done = bf16[128,256]{1,0:T(8,128)(2,1)} async-done(((bf16[1024,256]{1,0:T(8,128)(2,1)}), bf16[128,256]{1,0:T(8,128)(2,1)}) %reduce-scatter.37.cloned.1.call-update) | async-done | bytes 65552
  1240.3 35.8 %reduce-scatter.35.cloned.1.call-done = bf16[128,256]{1,0:T(8,128)(2,1)} async-done(((bf16[1024,256]{1,0:T(8,128)(2,1)}), bf16[128,256]{1,0:T(8,128)(2,1)}) %reduce-scatter.35.cloned.1.call-update) | async-done | bytes 65552 | tf_op jit(solution)/shard_map/reduce_scatter | solution.py:353
  1277.6 35.5 %reduce-scatter.29.cloned.1.call-done = bf16[128,256]{1,0:T(8,128)(2,1)} async-done(((bf16[1024,256]{1,0:T(8,128)(2,1)}), bf16[128,256]{1,0:T(8,128)(2,1)}) %reduce-scatter.29.cloned.1.call-update) | async-done | bytes 65552 | tf_op jit(solution)/shard_map/reduce_scatter | solution.py:344
  1314.7 35.9 %reduce-scatter.31.cloned.1.call-done = bf16[128,256]{1,0:T(8,128)(2,1)} async-done(((bf16[1024,256]{1,0:T(8,128)(2,1)}), bf16[128,256]{1,0:T(8,128)(2,1)}) %reduce-scatter.31.cloned.1.call-update) | async-done | bytes 65552 | tf_op jit(solution)/shard_map/reduce_scatter | solution.py:347
  1352.1 35.5 %reduce-scatter.33.cloned.1.call-done = bf16[128,256]{1,0:T(8,128)(2,1)} async-done(((bf16[1024,256]{1,0:T(8,128)(2,1)}), bf16[128,256]{1,0:T(8,128)(2,1)}) %reduce-scatter.33.cloned.1.call-update) | async-done | bytes 65552 | tf_op jit(solution)/shard_map/reduce_scatter | solution.py:350
  1389.1 80.8 %all-gather.17.cloned.1.call-done = bf16[2048,1024]{1,0:T(8,128)(2,1)} async-done(((bf16[512,1024]{1,0:T(8,128)(2,1)}), bf16[2048,1024]{1,0:T(8,128)(2,1)}) %all-gather.17.cloned.1.call-update) | async-done | bytes 4194320 | tf_op jit(solution)/shard_map/all_gather | solution.py:332
  1469.9 6.2 fusion.11
  1476.1 25.1 %all-reduce.5 = (f32[1024]{0:T(1024)}, f32[3,4,256]{2,0,1:T(4,128)S(1)}, f32[16,256]{1,0:T(8,128)}, f32[16,256]{1,0:T(8,128)}, f32[1024]{0:T(1024)}) all-reduce(f32[1024]{0:T(1024)S(1)} %get-tuple-element.444, f32[3,4,256]{2,0,1:T(4,128)S(1)} %pad_maximum_fusion.9, ...), channel_id=1, replica_groups=mesh['seq'=8,'head'=4] {'seq'}, use_global_device_ids=true, to_apply=%region_22.23 | all-reduce | flops 13312 | bytes 106496 | tf_op jit(solution)/shard_map/psum | solution.py:340
  1501.9 9.0 fusion.7
  (383 shorter events, 264.0 us)
Async XLA Ops:
  7.2 444.1 %copy-start = (bf16[704,1024]{1,0:T(8,128)(2,1)S(1)}, bf16[704,1024]{1,0:T(8,128)(2,1)}, u32[]{:S(2)}) copy-start(bf16[704,1024]{1,0:T(8,128)(2,1)} %param.36) | copy-start | bytes 4325380
  7.2 93.8 %all-gather.19.cloned.1.call-start = ((), (), s32[]{:S(2)}) async-start(), calls=%async_computation.24 | async-start | bytes 4718592 | tf_op jit(solution)/shard_map/all_gather | solution.py:24
  17.6 3.5 collective-permute-start
  20.9 20.4 %copy-start.73 = (bf16[4,512]{1,0:T(4,128)(2,1)}, bf16[4,512]{1,0:T(4,128)(2,1)S(1)}, u32[]{:S(2)}) copy-start(bf16[4,512]{1,0:T(4,128)(2,1)S(1)} %get-tuple-element.511) | copy-start | bytes 12292
  42.3 30.3 %copy-start.22 = (bf16[4,512,2,128]{3,2,1,0:T(2,128)(2,1)S(1)}, bf16[4,512,2,128]{3,2,1,0:T(2,128)(2,1)}, u32[]{:S(2)}) copy-start(bf16[4,512,2,128]{3,2,1,0:T(2,128)(2,1)} %convert_element_type.178) | copy-start | bytes 3145732
  45.3 235.4 %reduce-scatter.21.cloned.1.call-start = ((), (), s32[]{:S(2)}) async-start(), calls=%async_computation.12 | async-start | bytes 10485760 | tf_op jit(solution)/shard_map/reduce_scatter | solution.py:190
  120.9 311.8 %all-gather.11.cloned.1.call-start = ((), (), s32[]{:S(2)}) async-start(), calls=%async_computation.13 | async-start | bytes 10485760 | tf_op jit(solution)/shard_map/all_gather | solution.py:191
  280.7 331.2 %reduce-scatter.25.cloned.1.call-start = ((), (), s32[]{:S(2)}) async-start(), calls=%async_computation.16 | async-start | bytes 10485760 | tf_op jit(solution)/shard_map/reduce_scatter | solution.py:224
  469.0 294.7 %all-gather.15.cloned.1.call-start = ((), (), s32[]{:S(2)}) async-start(), calls=%async_computation.17 | async-start | bytes 10485760 | tf_op jit(solution)/shard_map/all_gather | solution.py:225
  611.9 223.7 %all-gather.21.cloned.1.call-start = ((), (), s32[]{:S(2)}) async-start(), calls=%async_computation.25 | async-start | bytes 4718592 | tf_op jit(solution)/shard_map/all_gather | solution.py:24
  763.7 11.9 copy-start.60
  800.5 144.3 %reduce-scatter.23.cloned.1.call-start = ((), (), s32[]{:S(2)}) async-start(), calls=%async_computation.14 | async-start | bytes 5242880 | tf_op jit(solution)/shard_map/reduce_scatter | solution.py:203
  807.4 187.5 %reduce-scatter.27.cloned.1.call-start = ((), (), s32[]{:S(2)}) async-start(), calls=%async_computation.18 | async-start | bytes 5242880 | tf_op jit(solution)/shard_map/reduce_scatter | solution.py:329
  809.0 12.6 slice-start.2
  809.0 12.6 slice-start.3
  870.9 14.1 copy-start.64
  870.9 14.1 copy-start.66
  870.9 14.1 copy-start.68
  870.9 14.1 copy-start.70
  889.7 3.1 collective-permute-start.1
  914.3 122.9 %reduce-scatter.43.cloned.1.call-start = ((), (), s32[]{:S(2)}) async-start(), calls=%async_computation.29 | async-start | bytes 1769472
  924.4 154.5 %reduce-scatter.41.cloned.1.call-start = ((), (), s32[]{:S(2)}) async-start(), calls=%async_computation.28 | async-start | bytes 1769472
  934.5 186.2 %reduce-scatter.39.cloned.1.call-start = ((), (), s32[]{:S(2)}) async-start(), calls=%async_computation.27 | async-start | bytes 1769472
  944.7 258.6 %all-gather.13.cloned.1.call-start = ((), (), s32[]{:S(2)}) async-start(), calls=%async_computation.15 | async-start | bytes 5242880 | tf_op jit(solution)/shard_map/all_gather | solution.py:210
  948.0 290.7 %reduce-scatter.37.cloned.1.call-start = ((), (), s32[]{:S(2)}) async-start(), calls=%async_computation.26 | async-start | bytes 589824
  956.0 320.1 %reduce-scatter.35.cloned.1.call-start = ((), (), s32[]{:S(2)}) async-start(), calls=%async_computation.23 | async-start | bytes 589824 | tf_op jit(solution)/shard_map/reduce_scatter | solution.py:353
  960.7 352.4 %reduce-scatter.29.cloned.1.call-start = ((), (), s32[]{:S(2)}) async-start(), calls=%async_computation.20 | async-start | bytes 589824 | tf_op jit(solution)/shard_map/reduce_scatter | solution.py:344
  965.1 385.5 %reduce-scatter.31.cloned.1.call-start = ((), (), s32[]{:S(2)}) async-start(), calls=%async_computation.21 | async-start | bytes 589824 | tf_op jit(solution)/shard_map/reduce_scatter | solution.py:347
  969.4 418.2 %reduce-scatter.33.cloned.1.call-start = ((), (), s32[]{:S(2)}) async-start(), calls=%async_computation.22 | async-start | bytes 589824 | tf_op jit(solution)/shard_map/reduce_scatter | solution.py:350
  973.9 496.1 %copy-start.53 = (f32[4,512]{1,0:T(4,128)S(1)}, f32[4,512]{1,0:T(4,128)}, u32[]{:S(2)}) copy-start(f32[4,512]{1,0:T(4,128)} %copy-done.52) | copy-start | bytes 24580
  973.9 496.1 %copy-start.62 = (f32[1024]{0:T(1024)S(1)}, f32[1024]{0:T(1024)}, u32[]{:S(2)}) copy-start(f32[1024]{0:T(1024)} %param.24) | copy-start | bytes 12292
  973.9 496.0 %all-gather.17.cloned.1.call-start = ((), (), s32[]{:S(2)}) async-start(), calls=%async_computation.19 | async-start | bytes 5242880 | tf_op jit(solution)/shard_map/all_gather | solution.py:332
  (75 other events, 312.7 us)
Sparse Core Ops, SparseCore 0:
  45.4 41.3 all-gather.18
  121.0 159.6 reduce-scatter.20
  282.3 150.3 all-gather.10
  469.1 142.6 reduce-scatter.24
  613.3 150.3 all-gather.14
  800.6 34.9 all-gather.20
  838.4 76.7 reduce-scatter.22
  917.6 77.2 reduce-scatter.26
  998.2 38.9 reduce-scatter.42
  1040.4 38.4 reduce-scatter.40
  1082.2 38.4 reduce-scatter.38
  1122.7 80.5 all-gather.12
  1206.3 32.2 reduce-scatter.36
  1241.9 34.1 reduce-scatter.34
  1279.0 34.0 reduce-scatter.28
  1316.4 34.1 reduce-scatter.30
  1353.5 34.0 reduce-scatter.32
  1389.1 80.7 all-gather.16
where the time goes:
time: 1530 us; the launch traced here: 1520 us
  waiting for transfers between devices  1090 us (71%)
  matrix products  151 us (10%)
  other arithmetic  124 us (8%)
  local copies, waits for them, and re-layouts  87.1 us (6%)
  blocking collectives  46.6 us (3%)
  between operations  16.1 us (1%)
    reduce_scatter x1, waiting for transfers between devices, local(): lax.psum_scatter(attn_part, 'head', scatter_dimension=0, tiled=True)  160 us
    unnamed x22, waiting for transfers between devices  156 us
    all_gather x1, waiting for transfers between devices, local(): attn_part = lax.all_gather(attn_share, 'head', axis=0, tiled=True)  152 us
    all_gather x1, waiting for transfers between devices, local(): two_part = lax.all_gather(two_share, 'head', axis=0, tiled=True)  152 us
    reduce_scatter x1, waiting for transfers between devices, local(): lax.psum_scatter(two_part, 'head', scatter_dimension=0, tiled=True)  143 us
    all_gather x1, waiting for transfers between devices, local(): lax.all_gather(one_share.astype(jnp.bfloat16), 'head', axis=0, tiled=True)  80.8 us
    all_gather x1, waiting for transfers between devices, local(): lax.all_gather((middle_share + live_three * shares).astype(jnp.bfloat16),...  80.7 us
    reduce_scatter x1, waiting for transfers between devices, local(): lax.psum_scatter(grad_key.astype(jnp.bfloat16), 'seq', scatter_dimension=...  35.9 us
  transfers between devices with their start and end apart: 20, of which 18 were waited for; matrix products, arithmetic and copies ran while one was open for 14% of the time, Pallas kernels for 0%

commit v1 on v0

v1 whole, which is shorter than its diff:
```python
import jax
import jax.numpy as jnp
from jax import lax
from jax.sharding import PartitionSpec as P

DH = 128
KW = 4
HALO = 8
EPSILON = 1e-06
BF = jnp.bfloat16
F32 = jnp.float32


def custom_mesh():
    return lax.axis_size("seq") == 8 and lax.axis_size("head") == 4


def along_seq(value, flip):
    return lax.ppermute(value, "seq", [(i, i ^ flip) for i in range(8)])


def along_head(value, pairs):
    return lax.ppermute(value, "head", pairs)


def slot_owner(k):
    return lax.axis_index("head") ^ k if custom_mesh() else k


def gather_head(value):
    z = lax.axis_index("head")
    middle = (z == 1) | (z == 2)
    one = along_head(value, [(0, 1), (1, 0), (2, 3), (3, 2)])
    inner = along_head(value, [(1, 2), (2, 1)])
    two_inner = along_head(one, [(1, 2), (2, 1)])
    two_outer = along_head(inner, [(2, 3), (1, 0)])
    three_outer = along_head(two_inner, [(2, 3), (1, 0)])
    two = jnp.where(middle, two_inner, two_outer)
    three = jnp.where(middle, inner, three_outer)
    return [value, one, two, three]


def gather_plane(value, x_first):
    near, far = (2, 4) if x_first else (4, 2)
    pieces = {0: value, near: along_seq(value, near), far: along_seq(value, far)}
    pieces[6] = along_seq(pieces[near], far)
    for j in (0, 2, 4, 6):
        pieces[j + 1] = along_seq(pieces[j], 1)
    return [pieces[j] for j in range(8)]


def gather_weights(own):
    if not custom_mesh():
        whole = lax.all_gather(own, "head")
        return [whole[k] for k in range(lax.axis_size("head"))]
    p = lax.axis_index("seq")
    matrices, depth, width = own.shape
    block = depth // 8
    mine = lax.dynamic_slice_in_dim(own, p * block, block, 1)
    slots = [own]
    for k, piece in enumerate(gather_head(mine)[1:]):
        if k < 2:
            parts = gather_plane(piece, k == 0)
        else:
            half = block // 2
            upper = gather_plane(piece[:, :half], True)
            lower = gather_plane(piece[:, half:], False)
            parts = [jnp.concatenate([u, v], axis=1) for u, v in zip(upper, lower)]
        full = jnp.zeros((matrices, depth, width), own.dtype)
        for j, part in enumerate(parts):
            full = lax.dynamic_update_slice_in_dim(full, part, (p ^ j) * block, 1)
        slots.append(full)
    return slots


def gather_small(own):
    if not custom_mesh():
        whole = lax.all_gather(own, "head")
        return [whole[k] for k in range(lax.axis_size("head"))]
    return [own] + [along_head(own, [(i, i ^ k) for i in range(4)]) for k in (1, 2, 3)]


def gather_states(value):
    p = lax.axis_index("seq")
    if not custom_mesh():
        whole = lax.all_gather(value, "seq")
        count = lax.axis_size("seq")
        return [whole[i] for i in range(count)], list(range(count))
    half = value.shape[0] // 2
    upper = gather_plane(value[:half], True)
    lower = gather_plane(value[half:], False)
    pieces = [jnp.concatenate([u, v]) for u, v in zip(upper, lower)]
    return pieces, [p ^ j for j in range(8)]


def gather_rows(own):
    if not custom_mesh():
        return lax.all_gather(own, "head")
    z = lax.axis_index("head")
    full = jnp.zeros((4,) + own.shape, own.dtype)
    for k, slot in enumerate(gather_head(own)):
        full = lax.dynamic_update_slice_in_dim(full, slot[None], z ^ k, 0)
    return full


def weight_grads(pairs, x_first):
    dot = lambda a, b: lax.dot_general(a, b, (((0,), (0,)), ((), ())), preferred_element_type=F32)
    if not custom_mesh():
        out = []
        for a, b in pairs:
            full = jnp.stack([dot(a, one) for one in b]).astype(BF)
            part = lax.psum_scatter(full, "head", scatter_dimension=0, tiled=True)[0]
            out.append(lax.psum_scatter(part, "seq", scatter_dimension=0, tiled=True).astype(F32))
        return out
    p, z = lax.axis_index("seq"), lax.axis_index("head")
    block = pairs[0][0].shape[1] // 8
    stacks = [[] for _ in range(4)]
    for a, b in pairs:
        cut = lambda j: lax.dynamic_slice_in_dim(a, (p ^ j) * block, block, 1)
        even = jnp.concatenate([cut(j) for j in (0, 2, 4, 6)], axis=1)
        odd = jnp.concatenate([cut(j) for j in (1, 3, 5, 7)], axis=1)
        peer_a = along_seq(odd, 1)
        for k in range(4):
            peer_b = along_seq(b[k], 1)
            stacks[k].append(
                (dot(even, b[k]) + dot(peer_a, peer_b)).astype(BF).reshape(4, block, -1)
            )
    near, far = (2, 4) if x_first else (4, 2)
    slots = []
    for k in range(4):
        g = jnp.stack(stacks[k])
        y_zero, y_one = g[:, :2], g[:, 2:]
        if x_first:
            keep = jnp.stack([g[:, 0], g[:, 2]], 1)
            away = jnp.stack([g[:, 1], g[:, 3]], 1)
        else:
            keep, away = y_zero, y_one
        summed = (keep.astype(F32) + along_seq(away, near).astype(F32)).astype(BF)
        slots.append(
            (summed[:, 0].astype(F32) + along_seq(summed[:, 1], far).astype(F32)).astype(BF)
        )
    return list(reduce_head(slots))


def add(a, b):
    return (a.astype(F32) + b.astype(F32)).astype(BF)


def reduce_head(slots):
    outer, inner, back = [(0, 1), (3, 2)], [(1, 2), (2, 1)], [(2, 3), (1, 0)]
    own, one, two, three = slots
    far = add(two, along_head(three, outer))
    far = add(one, along_head(far, inner))
    far = along_head(far, back)
    mid = add(three, along_head(two, outer))
    mid = along_head(mid, inner)
    near = along_head(one, outer)
    return own.astype(F32) + far.astype(F32) + mid.astype(F32) + near.astype(F32)


def sum_small(slots, gains):
    if not custom_mesh():
        part = lax.psum_scatter(jnp.stack(slots), "head", scatter_dimension=0, tiled=True)[0]
        return lax.psum(part, "seq"), lax.psum(gains, ("seq", "head"))
    part = slots[0]
    for k in (1, 2, 3):
        part = part + along_head(slots[k], [(i, i ^ k) for i in range(4)])
    for k in (1, 2):
        gains = gains + along_head(gains, [(i, i ^ k) for i in range(4)])
    count = part.shape[0]
    total = jnp.concatenate([part, gains])
    for flip in (1, 2, 4):
        total = total + along_seq(total, flip)
    return total[:count], total[count:]


def norm_keep(values):
    inverse = lax.rsqrt(jnp.mean(values * values, axis=-1, keepdims=True) + EPSILON)
    return (values * inverse, inverse)


def norm_back(grad, normed, inverse):
    return inverse * (grad - normed * jnp.mean(grad * normed, axis=-1, keepdims=True))


def silu_slope(values):
    sigma = jax.nn.sigmoid(values)
    return sigma * (1.0 + values * (1.0 - sigma))


def carry_coefficients(alpha, eta):
    count, heads = alpha.shape
    place = jnp.arange(count)[:, None]
    mem = jnp.zeros((count, heads), F32)
    mom = jnp.zeros((count, heads), F32)
    rows = []
    for c in range(count):
        rows.append(mem)
        mom = eta[c] * mom + (place == c).astype(F32)
        mem = alpha[c] * mem + mom
    return jnp.stack(rows)


def dot(a, b):
    return jnp.dot(a, b, preferred_element_type=F32)


def dot_t(a, b):
    return lax.dot_general(a, b, (((1,), (1,)), ((), ())), preferred_element_type=F32)


def local(
    inputs,
    lengths,
    decays,
    norm_gain,
    query_proj,
    key_proj,
    value_proj,
    gate_proj,
    conv_taps,
    pers_keys,
    pers_values,
    out_proj,
    ffn_gain,
    ffn_gate,
    ffn_up,
    ffn_down,
    cotangent,
):
    seqs, seg, features = inputs.shape
    segments = lax.axis_size("seq")
    shards = lax.axis_size("head")
    p, z = lax.axis_index("seq"), lax.axis_index("head")
    width = query_proj.shape[1]
    heads_here = width // DH
    heads = heads_here * shards
    rim = KW - 1
    persistent = pers_keys.shape[0]

    attn_slots = gather_weights(jnp.stack([query_proj, key_proj, value_proj, gate_proj, out_proj.T]))
    ffn_slots = gather_weights(jnp.stack([ffn_gate, ffn_up, ffn_down.T]))
    small = gather_small(
        jnp.concatenate([conv_taps.reshape(3 * KW, width), pers_keys, pers_values])
    )
    small = jnp.concatenate(small, axis=1)
    taps = small[: 3 * KW].reshape(3, KW, heads * DH).astype(F32)
    pers_k = small[3 * KW : 3 * KW + persistent].reshape(persistent, heads, DH)
    pers_v = small[3 * KW + persistent :].reshape(persistent, heads, DH)
    q_mat, k_mat, v_mat, g_mat, o_mat = [
        jnp.concatenate([slot[i] for slot in attn_slots], axis=1) for i in range(5)
    ]

    mine = lax.dynamic_index_in_dim(decays, z, 1, False)[:, 0]
    mine = jnp.concatenate(
        [lax.dynamic_slice_in_dim(mine, slot_owner(k) * heads_here, heads_here, 1) for k in range(shards)],
        axis=1,
    )
    every = lax.all_gather(mine, "seq")
    carry = carry_coefficients(every[:, 0], every[:, 1])

    x = lax.dynamic_index_in_dim(inputs, z, 0, False).astype(F32)
    cot = lax.dynamic_index_in_dim(cotangent, z, 0, False).astype(F32)
    length = lax.dynamic_index_in_dim(lengths, z, 0, False)
    live = ((p * seg + jnp.arange(seg, dtype=jnp.int32)) < length).astype(F32)
    live_two = live[:, None]
    tail = lax.dynamic_index_in_dim(inputs, z, 0, False)[seg - HALO :]
    before = lax.ppermute(tail, "seq", [(i, i + 1) for i in range(segments - 1)]).astype(F32)
    x_long = jnp.concatenate([before, x])
    n_long, inv_long = norm_keep(x_long)
    h_long = (n_long * norm_gain).astype(BF)
    n_one, inv_one, h_one = n_long[HALO:], inv_long[HALO:], h_long[HALO:]

    pre = jnp.stack([dot(h_long, m) for m in (q_mat, k_mat, v_mat)]).astype(BF)
    zgate = dot(h_one, g_mat)
    wide_pre = pre.astype(F32)
    conv_sum = sum(
        taps[:, lag][:, None, :] * wide_pre[:, HALO - lag : HALO - lag + seg] for lag in range(KW)
    )
    acts = jax.nn.silu(conv_sum).reshape(3, seg, heads, DH)
    q_normed, q_inverse = norm_keep(acts[0])
    k_normed, k_inverse = norm_keep(acts[1])
    query, keyed, valued = q_normed.astype(BF), k_normed.astype(BF), acts[2].astype(BF)
    live_three = live[:, None, None]
    masked_value = valued * live_three.astype(BF)
    write = jnp.einsum("tha,thb->hab", masked_value, keyed, preferred_element_type=F32) / seg

    def mix_states(values, coefficients):
        pieces, places = gather_states(values.astype(BF))
        total = 0.0
        for piece, place in zip(pieces, places):
            coefficient = lax.dynamic_index_in_dim(coefficients, place, 0, False)
            total = total + coefficient[:, None, None] * piece.astype(F32)
        return total.astype(BF)

    prior = mix_states(write, lax.dynamic_index_in_dim(carry, p, 0, False))
    raw_read = jnp.einsum("hab,thb->tha", prior, query, preferred_element_type=F32)
    readout, read_inverse = norm_keep(raw_read)

    keys_all = jnp.concatenate([pers_k, keyed])
    values_all = jnp.concatenate([pers_v, valued])
    valid = jnp.concatenate([jnp.ones((persistent,), F32), live])
    rows_index = jnp.arange(seg)[:, None]
    column = jnp.arange(persistent + seg)[None, :] - persistent
    allowed = (column < 0) | (column <= rows_index) & (valid[None, :] > 0.5)
    scale = DH ** (-0.5)
    score = jnp.einsum("thd,uhd->htu", query, keys_all, preferred_element_type=F32) * scale
    score = jnp.where(allowed[None], score, -1e30)
    top = jnp.max(score, axis=-1, keepdims=True)
    log_total = top + jnp.log(jnp.sum(jnp.exp(score - top), axis=-1, keepdims=True))
    prob = jnp.exp(score - log_total)
    prob_low = prob.astype(BF)
    attended = jnp.einsum("htu,uhd->thd", prob_low, values_all, preferred_element_type=F32)

    sigma = jax.nn.sigmoid(zgate)
    read_flat = readout.reshape(seg, -1)
    mixed = (attended.reshape(seg, -1) + sigma * read_flat).astype(BF)
    middle = x + live_two * dot_t(mixed, o_mat)
    n_two, inv_two = norm_keep(middle)
    h_two = (n_two * ffn_gain).astype(BF)

    gffn = (live_two * cot).astype(BF)
    ffn_out = 0.0
    dh_two = 0.0
    hidden_slots, gate_slots, up_slots = [], [], []
    for slot in ffn_slots:
        gate_value = dot(h_two, slot[0])
        up_value = dot(h_two, slot[1])
        silu_gate = jax.nn.silu(gate_value)
        hidden = (silu_gate * up_value).astype(BF)
        ffn_out = ffn_out + dot_t(hidden, slot[2])
        dhidden = dot(gffn, slot[2])
        dgate = (dhidden * up_value * silu_slope(gate_value)).astype(BF)
        dup = (dhidden * silu_gate).astype(BF)
        dh_two = dh_two + dot_t(dgate, slot[0]) + dot_t(dup, slot[1])
        hidden_slots.append(hidden)
        gate_slots.append(dgate)
        up_slots.append(dup)
    output = gather_rows((middle + live_two * ffn_out).astype(BF))
    g_gate, g_up, g_down = weight_grads(
        [(h_two, gate_slots), (h_two, up_slots), (gffn, hidden_slots)], True
    )

    grad_ffn_gain = jnp.sum(dh_two * n_two, axis=0)
    dmiddle = cot + norm_back(dh_two * ffn_gain, n_two, inv_two)
    gattn = (live_two * dmiddle).astype(BF)
    dmixed = dot(gattn, o_mat)
    datt = dmixed.astype(BF).reshape(seg, heads, DH)
    dzgate = (dmixed * read_flat * sigma * (1.0 - sigma)).astype(BF)
    dread = norm_back((dmixed * sigma).reshape(seg, heads, DH), readout, read_inverse).astype(BF)
    dprior = jnp.einsum("tha,thb->hab", dread, query, preferred_element_type=F32)
    dwrite = mix_states(dprior, lax.dynamic_index_in_dim(carry, p, 1, False))
    dquery_mem = jnp.einsum("hab,tha->thb", prior, dread, preferred_element_type=F32)
    dprob = jnp.einsum("thd,uhd->htu", datt, values_all, preferred_element_type=F32)
    row_dot = jnp.sum(prob * dprob, axis=-1, keepdims=True)
    dscore = (prob * (dprob - row_dot)).astype(BF)
    dquery = (
        jnp.einsum("htu,uhd->thd", dscore, keys_all, preferred_element_type=F32) * scale
        + dquery_mem
    )
    dkeys = jnp.einsum("htu,thd->uhd", dscore, query, preferred_element_type=F32) * scale
    dvalues = jnp.einsum("htu,thd->uhd", prob_low, datt, preferred_element_type=F32)
    dvals = (
        dvalues[persistent:]
        + live_three * jnp.einsum("hab,thb->tha", dwrite, keyed, preferred_element_type=F32) / seg
    )
    dkey = (
        dkeys[persistent:]
        + jnp.einsum("hab,tha->thb", dwrite, masked_value, preferred_element_type=F32) / seg
    )
    dact = jnp.stack(
        [norm_back(dquery, q_normed, q_inverse), norm_back(dkey, k_normed, k_inverse), dvals]
    ).reshape(3, seg, -1)
    dconv = dact * silu_slope(conv_sum)
    longer = jnp.pad(dconv, ((0, 0), (rim, rim), (0, 0)))
    spread = sum(
        taps[:, lag][:, None, :] * longer[:, lag : lag + seg + rim] for lag in range(KW)
    )
    grad_conv = jnp.stack(
        [
            jnp.sum(dconv * wide_pre[:, HALO - lag : HALO - lag + seg], axis=1)
            for lag in range(KW)
        ],
        axis=1,
    )
    back = lax.ppermute(
        spread[:, :rim].astype(BF), "seq", [(i + 1, i) for i in range(segments - 1)]
    ).astype(F32)
    dpre = spread[:, rim:] + jnp.pad(back, ((0, 0), (seg - rim, 0), (0, 0)))
    dpre = dpre.astype(BF)

    dh_one = (
        dot_t(dpre[0], q_mat) + dot_t(dpre[1], k_mat) + dot_t(dpre[2], v_mat) + dot_t(dzgate, g_mat)
    )
    grad_norm_gain = jnp.sum(dh_one * n_one, axis=0)
    input_grad = gather_rows(
        (dmiddle + norm_back(dh_one * norm_gain, n_one, inv_one)).astype(BF)
    )

    def by_slot(value):
        return [value[..., k * width : (k + 1) * width] for k in range(shards)]

    g_query, g_key, g_value, g_zgate, g_out = weight_grads(
        [(h_one, by_slot(d)) for d in (dpre[0], dpre[1], dpre[2], dzgate)]
        + [(gattn, by_slot(mixed))],
        False,
    )
    rows = jnp.concatenate(
        [
            grad_conv.reshape(3 * KW, -1),
            dkeys[:persistent].reshape(persistent, -1),
            dvalues[:persistent].reshape(persistent, -1),
        ]
    )
    gains = jnp.concatenate([grad_norm_gain, grad_ffn_gain]).reshape(-1, width)
    rows, gains = sum_small(by_slot(rows), gains)
    gains = gains.reshape(2, features)
    return (
        output,
        input_grad,
        gains[0],
        g_query,
        g_key,
        g_value,
        g_zgate,
        rows[: 3 * KW].reshape(3, KW, width),
        rows[3 * KW : 3 * KW + persistent],
        rows[3 * KW + persistent :],
        g_out.T,
        gains[1],
        g_gate,
        g_up,
        g_down.T,
    )


def solution(mesh):
    in_specs = (
        P(None, "seq", None),
        P(),
        P(None, None, "seq", None),
        P(),
        P(None, "head"),
        P(None, "head"),
        P(None, "head"),
        P(None, "head"),
        P(None, None, "head"),
        P(None, "head"),
        P(None, "head"),
        P("head", None),
        P(),
        P(None, "head"),
        P(None, "head"),
        P("head", None),
        P(None, "seq", None),
    )
    out_specs = (
        P(None, "seq", None),
        P(None, "seq", None),
        P(),
        P("seq", "head"),
        P("seq", "head"),
        P("seq", "head"),
        P("seq", "head"),
        P(None, None, "head"),
        P(None, "head"),
        P(None, "head"),
        P("head", "seq"),
        P(),
        P("seq", "head"),
        P("seq", "head"),
        P("head", "seq"),
    )
    return jax.shard_map(local, mesh=mesh, in_specs=in_specs, out_specs=out_specs, check_vma=False)
```

time: 1530 us -> 953 us (0.62)
  waiting for transfers between devices: 1090 us -> 212 us
  starting transfers between devices: 6.09 us -> 167 us
  local copies, waits for them, and re-layouts: 87.1 us -> 217 us
  matrix products: 151 us -> 223 us
  blocking collectives: 46.6 us -> 9.52 us
    all_gather x6 -> x0, waiting for transfers between devices: 467 us -> none  [the longest x1 152 us: local(): attn_part = lax.all_gather(attn_share, 'head', axis=0, tiled=True)]
    reduce_scatter x8 -> x0, waiting for transfers between devices: 466 us -> none  [the longest x1 160 us: local(): lax.psum_scatter(attn_part, 'head', scatter_dimension=0, tiled=True)]
    ppermute x2 -> x181, waiting for transfers between devices: 0.94 us -> 212 us  [the longest x139 133 us: along_seq(): return lax.ppermute(value, 'seq', [(i, i ^ flip) for i in range(8)])]
    ppermute x2 -> x181, starting transfers between devices: 4.64 us -> 167 us  [the longest x139 83 us: along_seq(): return lax.ppermute(value, 'seq', [(i, i ^ flip) for i in range(8)])]
    unnamed x22 -> x0, waiting for transfers between devices: 156 us -> none
    dot_general x36 -> x110, matrix products: 151 us -> 223 us  [the longest x64 97.2 us: weight_grads(): lax.dot_general(a, b, (((0,), (0,)), ((), ())), preferred_element_type=F32)]
    dynamic_update_slice x0 -> x38, local copies, waits for them, and re-layouts: none -> 44.1 us  [the longest x36 39.6 us: gather_weights(): full = lax.dynamic_update_slice_in_dim(full, part, (p ^ j) * block, 1)]
    another operation x6 -> x36, local copies, waits for them, and re-layouts: 19.1 us -> 48.9 us  [the longest x20 29.3 us: weight_grads(): g = jnp.stack(stacks[k])]
  transfers between devices with their start and end apart: 20 -> 181, of which waited for: 18 -> 38; matrix products, arithmetic and copies ran while one was open for 14% -> 54% of each run, Pallas kernels for 0% -> 0%
where the time goes in v1:
time: 953 us; the launch traced here: 944 us
  matrix products  223 us (23%)
  local copies, waits for them, and re-layouts  217 us (23%)
  waiting for transfers between devices  212 us (22%)
  starting transfers between devices  167 us (18%)
  other arithmetic  110 us (12%)
    ppermute x139, waiting for transfers between devices, along_seq(): return lax.ppermute(value, 'seq', [(i, i ^ flip) for i in range(8)])  133 us
    dot_general x64, matrix products, weight_grads(): lax.dot_general(a, b, (((0,), (0,)), ((), ())), preferred_element_type=F32)  97.2 us
    ppermute x139, starting transfers between devices, along_seq(): return lax.ppermute(value, 'seq', [(i, i ^ flip) for i in range(8)])  83 us
    ppermute x40, starting transfers between devices, along_head(): return lax.ppermute(value, 'head', pairs)  81.4 us
    ppermute x40, waiting for transfers between devices, along_head(): return lax.ppermute(value, 'head', pairs)  78.5 us
    unnamed x656, local copies, waits for them, and re-layouts  53 us
    dot_general x17, matrix products, dot_t(): lax.dot_general(a, b, (((1,), (1,)), ((), ())), preferred_element_type=F32)  47 us
    dot_general x17, matrix products, dot(): return jnp.dot(a, b, preferred_element_type=F32)  40.9 us
  transfers between devices with their start and end apart: 181, of which 38 were waited for; matrix products, arithmetic and copies ran while one was open for 54% of the time, Pallas kernels for 0%

profile of v1, /device:TPU:0, one launch (start us, length us, event | category | flops | bytes accessed | tf_op | source)
XLA Modules:
  0.0 944.2 jit_solution(11345754012122127265)
XLA Ops:
  24.7 9.5 %all-gather.1 = f32[8,2,8]{2,1,0:T(2,128)S(1)} all-gather(f32[1,2,8]{2,1,0:T(2,128)S(1)} %maximum_bitcast_fusion), channel_id=2, replica_groups=mesh['seq'=8,'head'=4] {'seq'}, dimensions={0}, use_global_device_ids=true | all-gather | bytes 576 | tf_op jit(solution)/shard_map/all_gather | solution.py:259
  59.1 8.3 collective-permute-done.51
  78.4 18.5 %collective-permute-done.22 = bf16[5,128,256]{1,2,0:T(8,128)(2,1)S(1)} collective-permute-done((bf16[5,128,256]{1,2,0:T(8,128)(2,1)S(1)}, bf16[5,128,256]{1,2,0:T(8,128)(2,1)S(1)}, u32[]{:S(2)}, u32[]{:S(2)}) %collective-permute-start.22) | collective-permute-done | bytes 327712 | tf_op jit(solution)/shard_map/ppermute | solution.py:23
  100.6 7.2 collective-permute-done.16
  114.8 8.5 collective-permute-done.53
  130.2 6.6 collective-permute-done.26
  145.3 4.2 collective-permute-done.20
  153.8 9.0 collective-permute-done.33
  200.7 5.7 fusion.2
  235.8 14.8 %fusion.132 = f32[8,128,512]{2,1,0:T(8,128)S(1)} fusion(bf16[528,8,128]{2,0,1:T(8,128)(2,1)S(1)} %copy_dynamic-update-slice_fusion, f32[8,512,528]{1,2,0:T(8,128)S(1)} %get-tuple-element.272, f32[8,512]{1,0:T(8,128)S(1)} %log_add_fusion, pred[512,528]{0,1:T(8,128)(4,1)S(1)} %fusion.61), kind=kOutput, calls=%fused_computation.572 | convolution fusion | flops 562298880 | bytes 12115968 | tf_op jit(solution)/shard_map/htu,uhd->thd/dot_general | solution.py:313
  273.1 5.9 add_convert_fusion.6
  324.6 3.8 fusion.31
  328.5 3.9 fusion.33
  332.3 4.3 collective-permute-done.80
  346.8 4.2 multiply_convert_fusion.11
  362.8 3.8 fusion.30
  420.5 4.1 multiply_reduce_fusion.6
  477.6 4.1 bitcast_dynamic-update-slice_fusion.7
  576.8 15.2 %multiply_reduce_fusion.4 = (f32[3,1024]{1,0:T(4,128)S(1)}, f32[3,1024]{1,0:T(4,128)S(1)}, f32[3,1024]{1,0:T(4,128)S(1)}, f32[3,1024]{1,0:T(4,128)S(1)}, f32[3,512,1024]{2,1,0:T(8,128)S(1)}) fusion(f32[3,520,1024]{2,1,0:T(8,128)} %copy-done, f32[3,512,1024]{2,1,0:T(8,128)} %get-tuple-element.99, f32[1,512,1024]{2,1,0:T(8,128)} %stack.148, ...), kind=kLoop, calls=%fused_computation.13 | loop fusion | flops 28299264 | bytes 44089344 | tf_op jit(solution)/shard_map/reduce_sum | solution.py:381
  601.9 3.8 fusion.1
  727.9 4.7 collective-permute-done.158
  736.9 18.1 %collective-permute-done.163 = bf16[3,2,128,704]{2,3,0,1:T(8,128)(2,1)} collective-permute-done((bf16[3,2,128,704]{2,3,0,1:T(8,128)(2,1)}, bf16[3,2,128,704]{2,3,0,1:T(8,128)(2,1)}, u32[]{:S(2)}, u32[]{:S(2)}) %collective-permute-start.163) | collective-permute-done | bytes 1081376 | tf_op jit(solution)/shard_map/ppermute | solution.py:19
  761.4 9.5 %collective-permute-done.145 = bf16[5,2,128,256]{3,2,0,1:T(8,128)(2,1)S(1)} collective-permute-done((bf16[5,2,128,256]{3,2,0,1:T(8,128)(2,1)S(1)}, bf16[5,2,128,256]{3,2,0,1:T(8,128)(2,1)S(1)}, u32[]{:S(2)}, u32[]{:S(2)}) %collective-permute-start.145) | collective-permute-done | bytes 655392 | tf_op jit(solution)/shard_map/ppermute | solution.py:19
  772.9 13.0 %collective-permute-done.131 = bf16[5,2,128,256]{3,2,0,1:T(8,128)(2,1)S(1)} collective-permute-done((bf16[5,2,128,256]{3,2,0,1:T(8,128)(2,1)S(1)}, bf16[5,2,128,256]{3,2,0,1:T(8,128)(2,1)S(1)}, u32[]{:S(2)}, u32[]{:S(2)}) %collective-permute-start.131) | collective-permute-done | bytes 655392 | tf_op jit(solution)/shard_map/ppermute | solution.py:19
  792.3 27.4 %collective-permute-done.146 = bf16[5,128,256]{2,1,0:T(8,128)(2,1)S(1)} collective-permute-done((bf16[5,128,256]{2,1,0:T(8,128)(2,1)S(1)}, bf16[5,128,256]{2,1,0:T(8,128)(2,1)S(1)}, u32[]{:S(2)}, u32[]{:S(2)}) %collective-permute-start.146) | collective-permute-done | bytes 327712 | tf_op jit(solution)/shard_map/ppermute | solution.py:19
  819.8 4.7 collective-permute-start.147
  830.8 4.4 collective-permute-start.150
  842.8 11.6 %collective-permute-done.87 = bf16[512,1024]{1,0:T(8,128)(2,1)S(1)} collective-permute-done((bf16[512,1024]{1,0:T(8,128)(2,1)}, bf16[512,1024]{1,0:T(8,128)(2,1)S(1)}, u32[]{:S(2)}, u32[]{:S(2)}) %collective-permute-start.87) | collective-permute-done | bytes 1048608 | tf_op jit(solution)/shard_map/ppermute | solution.py:23
  865.6 17.5 %collective-permute-start.152 = (bf16[5,128,256]{2,1,0:T(8,128)(2,1)S(1)}, bf16[5,128,256]{2,1,0:T(8,128)(2,1)S(1)}, u32[]{:S(2)}, u32[]{:S(2)}) collective-permute-start(bf16[5,128,256]{2,1,0:T(8,128)(2,1)S(1)} %get-tuple-element.88), channel_id=1, source_target_pairs={{0,1},{3,2},{4,5},{7,6},{8,9},{11,10},{12,13},{15,14},{16,17},{19,... | collective-permute-start | bytes 983048 | tf_op jit(solution)/shard_map/ppermute | solution.py:23
  896.8 3.9 collective-permute-done.164
  904.4 12.6 %collective-permute-done.88 = bf16[512,1024]{1,0:T(8,128)(2,1)} collective-permute-done((bf16[512,1024]{1,0:T(8,128)(2,1)}, bf16[512,1024]{1,0:T(8,128)(2,1)}, u32[]{:S(2)}, u32[]{:S(2)}) %collective-permute-start.88) | collective-permute-done | bytes 1048608 | tf_op jit(solution)/shard_map/ppermute | solution.py:23
  921.1 15.9 %collective-permute-done.108 = bf16[512,1024]{1,0:T(8,128)(2,1)} collective-permute-done((bf16[512,1024]{1,0:T(8,128)(2,1)}, bf16[512,1024]{1,0:T(8,128)(2,1)}, u32[]{:S(2)}, u32[]{:S(2)}) %collective-permute-start.108) | collective-permute-done | bytes 1048608 | tf_op jit(solution)/shard_map/ppermute | solution.py:23
  (1366 shorter events, 650.1 us)
Async XLA Ops:
  8.7 46.8 %collective-permute-start.4 = (bf16[5,128,256]{1,2,0:T(8,128)(2,1)}, bf16[5,128,256]{1,2,0:T(8,128)(2,1)}, u32[]{:S(2)}, u32[]{:S(2)}) collective-permute-start(bf16[5,128,256]{1,2,0:T(8,128)(2,1)} %constant_dynamic-slice_fusion.52), channel_id=1, source_target_pairs={{0,1},{1,0},{2,3},{3,2},{4,5},{5,4},{6,7},{7,6},{8,9},{9,8},{10,11... | collective-permute-start | bytes 983048 | tf_op jit(solution)/shard_map/ppermute | solution.py:23
  11.8 44.6 %collective-permute-start.13 = (bf16[5,128,256]{1,2,0:T(8,128)(2,1)}, bf16[5,128,256]{1,2,0:T(8,128)(2,1)}, u32[]{:S(2)}, u32[]{:S(2)}) collective-permute-start(bf16[5,128,256]{1,2,0:T(8,128)(2,1)} %constant_dynamic-slice_fusion.52), channel_id=1, source_target_pairs={{1,2},{2,1},{5,6},{6,5},{9,10},{10,9},{13,14},{14,13},{17,18},{18,... | collective-permute-start | bytes 983048 | tf_op jit(solution)/shard_map/ppermute | solution.py:23
  13.8 38.3 %collective-permute-start = (bf16[44,256]{1,0:T(8,128)(2,1)}, bf16[44,256]{1,0:T(8,128)(2,1)S(1)}, u32[]{:S(2)}, u32[]{:S(2)}) collective-permute-start(bf16[44,256]{1,0:T(8,128)(2,1)} %pad_maximum_fusion.42), channel_id=1, source_target_pairs={{0,1},{1,0},{2,3},{3,2},{4,5},{5,4},{6,7},{7,6},{8,9},{9,8},{10,11... | collective-permute-start | bytes 67592 | tf_op jit(solution)/shard_map/ppermute | solution.py:23
  74.1 36.4 %collective-permute-start.59 = (bf16[3,128,704]{1,2,0:T(8,128)(2,1)}, bf16[3,128,704]{1,2,0:T(8,128)(2,1)S(1)}, u32[]{:S(2)}, u32[]{:S(2)}) collective-permute-start(bf16[3,128,704]{1,2,0:T(8,128)(2,1)} %collective-permute-done.51), channel_id=1, source_target_pairs={{1,2},{2,1},{5,6},{6,5},{9,10},{10,9},{13,14},{14,13},{17,18},{18,... | collective-permute-start | bytes 1622024 | tf_op jit(solution)/shard_map/ppermute | solution.py:23
  181.6 52.2 %collective-permute-start.70 = (bf16[3,64,704]{2,1,0:T(8,128)(2,1)}, bf16[3,64,704]{2,1,0:T(8,128)(2,1)}, u32[]{:S(2)}, u32[]{:S(2)}) collective-permute-start(bf16[3,64,704]{2,1,0:T(8,128)(2,1)} %copy.369), channel_id=1, source_target_pairs={{0,4},{4,0},{8,12},{12,8},{16,20},{20,16},{24,28},{28,24},{1,5},{5... | collective-permute-start | bytes 811016 | tf_op jit(solution)/shard_map/ppermute | solution.py:19
  185.5 49.3 %collective-permute-start.71 = (bf16[3,64,704]{2,1,0:T(8,128)(2,1)}, bf16[3,64,704]{2,1,0:T(8,128)(2,1)}, u32[]{:S(2)}, u32[]{:S(2)}) collective-permute-start(bf16[3,64,704]{2,1,0:T(8,128)(2,1)} %copy.370), channel_id=1, source_target_pairs={{0,4},{4,0},{8,12},{12,8},{16,20},{20,16},{24,28},{28,24},{1,5},{5... | collective-permute-start | bytes 811016 | tf_op jit(solution)/shard_map/ppermute | solution.py:19
  265.2 56.4 %collective-permute-start.58 = (bf16[3,128,704]{1,2,0:T(8,128)(2,1)}, bf16[3,128,704]{1,2,0:T(8,128)(2,1)}, u32[]{:S(2)}, u32[]{:S(2)}) collective-permute-start(bf16[3,128,704]{1,2,0:T(8,128)(2,1)} %collective-permute-done.57), channel_id=1, source_target_pairs={{0,4},{4,0},{8,12},{12,8},{16,20},{20,16},{24,28},{28,24},{1,5},{5... | collective-permute-start | bytes 1622024 | tf_op jit(solution)/shard_map/ppermute | solution.py:19
  265.3 45.7 %collective-permute-start.74 = (bf16[3,64,704]{2,1,0:T(8,128)(2,1)}, bf16[3,64,704]{2,1,0:T(8,128)(2,1)}, u32[]{:S(2)}, u32[]{:S(2)}) collective-permute-start(bf16[3,64,704]{2,1,0:T(8,128)(2,1)} %collective-permute-done.72), channel_id=1, source_target_pairs={{0,4},{4,0},{8,12},{12,8},{16,20},{20,16},{24,28},{28,24},{1,5},{5... | collective-permute-start | bytes 811016 | tf_op jit(solution)/shard_map/ppermute | solution.py:19
  265.7 45.7 %collective-permute-start.75 = (bf16[3,64,704]{2,1,0:T(8,128)(2,1)}, bf16[3,64,704]{2,1,0:T(8,128)(2,1)}, u32[]{:S(2)}, u32[]{:S(2)}) collective-permute-start(bf16[3,64,704]{2,1,0:T(8,128)(2,1)} %collective-permute-done.73), channel_id=1, source_target_pairs={{0,4},{4,0},{8,12},{12,8},{16,20},{20,16},{24,28},{28,24},{1,5},{5... | collective-permute-start | bytes 811016 | tf_op jit(solution)/shard_map/ppermute | solution.py:19
  265.8 49.7 %collective-permute-start.79 = (bf16[3,64,704]{2,1,0:T(8,128)(2,1)}, bf16[3,64,704]{2,1,0:T(8,128)(2,1)}, u32[]{:S(2)}, u32[]{:S(2)}) collective-permute-start(bf16[3,64,704]{2,1,0:T(8,128)(2,1)} %collective-permute-done.77), channel_id=1, source_target_pairs={{0,4},{4,0},{8,12},{12,8},{16,20},{20,16},{24,28},{28,24},{1,5},{5... | collective-permute-start | bytes 811016 | tf_op jit(solution)/shard_map/ppermute | solution.py:19
  266.2 50.3 %collective-permute-start.78 = (bf16[3,64,704]{2,1,0:T(8,128)(2,1)}, bf16[3,64,704]{2,1,0:T(8,128)(2,1)}, u32[]{:S(2)}, u32[]{:S(2)}) collective-permute-start(bf16[3,64,704]{2,1,0:T(8,128)(2,1)} %collective-permute-done.76), channel_id=1, source_target_pairs={{0,4},{4,0},{8,12},{12,8},{16,20},{20,16},{24,28},{28,24},{1,5},{5... | collective-permute-start | bytes 811016 | tf_op jit(solution)/shard_map/ppermute | solution.py:19
  311.0 195.6 %collective-permute-start.156 = (bf16[512,512]{1,0:T(8,128)(2,1)}, bf16[512,512]{1,0:T(8,128)(2,1)}, u32[]{:S(2)}, u32[]{:S(2)}) collective-permute-start(bf16[512,512]{1,0:T(8,128)(2,1)} %pad_maximum_fusion.27), channel_id=1, source_target_pairs={{0,4},{4,0},{8,12},{12,8},{16,20},{20,16},{24,28},{28,24},{1,5},{5... | collective-permute-start | bytes 1572872 | tf_op jit(solution)/shard_map/ppermute | solution.py:19
  311.4 231.7 %collective-permute-start.117 = (bf16[512,512]{1,0:T(8,128)(2,1)}, bf16[512,512]{1,0:T(8,128)(2,1)S(1)}, u32[]{:S(2)}, u32[]{:S(2)}) collective-permute-start(bf16[512,512]{1,0:T(8,128)(2,1)} %pad_maximum_fusion.21), channel_id=1, source_target_pairs={{0,4},{4,0},{8,12},{12,8},{16,20},{20,16},{24,28},{28,24},{1,5},{5... | collective-permute-start | bytes 1572872 | tf_op jit(solution)/shard_map/ppermute | solution.py:19
  351.9 141.7 %collective-permute-start.155 = (bf16[512,704]{0,1:T(8,128)(2,1)}, bf16[512,704]{0,1:T(8,128)(2,1)}, u32[]{:S(2)}, u32[]{:S(2)}) collective-permute-start(bf16[512,704]{0,1:T(8,128)(2,1)} %get-tuple-element.116), channel_id=1, source_target_pairs={{0,4},{4,0},{8,12},{12,8},{16,20},{20,16},{24,28},{28,24},{1,5},{5... | collective-permute-start | bytes 2162696 | tf_op jit(solution)/shard_map/ppermute | solution.py:19
  370.2 128.8 %collective-permute-start.154 = (bf16[512,704]{0,1:T(8,128)(2,1)}, bf16[512,704]{0,1:T(8,128)(2,1)}, u32[]{:S(2)}, u32[]{:S(2)}) collective-permute-start(bf16[512,704]{0,1:T(8,128)(2,1)} %get-tuple-element.117), channel_id=1, source_target_pairs={{0,4},{4,0},{8,12},{12,8},{16,20},{20,16},{24,28},{28,24},{1,5},{5... | collective-permute-start | bytes 2162696 | tf_op jit(solution)/shard_map/ppermute | solution.py:19
  400.2 93.4 %collective-permute-start.153 = (bf16[512,512]{1,0:T(8,128)(2,1)}, bf16[512,512]{1,0:T(8,128)(2,1)S(1)}, u32[]{:S(2)}, u32[]{:S(2)}) collective-permute-start(bf16[512,512]{1,0:T(8,128)(2,1)} %pad_maximum_fusion.25), channel_id=1, source_target_pairs={{0,4},{4,0},{8,12},{12,8},{16,20},{20,16},{24,28},{28,24},{1,5},{5... | collective-permute-start | bytes 1572872 | tf_op jit(solution)/shard_map/ppermute | solution.py:19
  507.1 41.5 %collective-permute-start.96 = (bf16[4,128,128]{2,1,0:T(8,128)(2,1)S(1)}, bf16[4,128,128]{2,1,0:T(8,128)(2,1)}, u32[]{:S(2)}, u32[]{:S(2)}) collective-permute-start(bf16[4,128,128]{2,1,0:T(8,128)(2,1)S(1)} %copy-done.232), channel_id=1, source_target_pairs={{0,16},{4,20},{8,24},{12,28},{16,0},{20,4},{24,8},{28,12},{1,17},{... | collective-permute-start | bytes 393224 | tf_op jit(solution)/shard_map/ppermute | solution.py:19
  557.8 79.9 %collective-permute-start.171 = (bf16[512,704]{0,1:T(8,128)(2,1)}, bf16[512,704]{0,1:T(8,128)(2,1)}, u32[]{:S(2)}, u32[]{:S(2)}) collective-permute-start(bf16[512,704]{0,1:T(8,128)(2,1)} %get-tuple-element.123), channel_id=1, source_target_pairs={{0,4},{4,0},{8,12},{12,8},{16,20},{20,16},{24,28},{28,24},{1,5},{5... | collective-permute-start | bytes 2162696 | tf_op jit(solution)/shard_map/ppermute | solution.py:19
  557.9 84.5 %collective-permute-start.170 = (bf16[512,704]{0,1:T(8,128)(2,1)}, bf16[512,704]{0,1:T(8,128)(2,1)}, u32[]{:S(2)}, u32[]{:S(2)}) collective-permute-start(bf16[512,704]{0,1:T(8,128)(2,1)} %get-tuple-element.122), channel_id=1, source_target_pairs={{0,4},{4,0},{8,12},{12,8},{16,20},{20,16},{24,28},{28,24},{1,5},{5... | collective-permute-start | bytes 2162696 | tf_op jit(solution)/shard_map/ppermute | solution.py:19
  663.8 45.2 %collective-permute-start.166 = (bf16[512,704]{0,1:T(8,128)(2,1)}, bf16[512,704]{0,1:T(8,128)(2,1)}, u32[]{:S(2)}, u32[]{:S(2)}) collective-permute-start(bf16[512,704]{0,1:T(8,128)(2,1)} %get-tuple-element.120), channel_id=1, source_target_pairs={{0,4},{4,0},{8,12},{12,8},{16,20},{20,16},{24,28},{28,24},{1,5},{5... | collective-permute-start | bytes 2162696 | tf_op jit(solution)/shard_map/ppermute | solution.py:19
  664.3 41.0 %collective-permute-start.165 = (bf16[512,704]{0,1:T(8,128)(2,1)}, bf16[512,704]{0,1:T(8,128)(2,1)}, u32[]{:S(2)}, u32[]{:S(2)}) collective-permute-start(bf16[512,704]{0,1:T(8,128)(2,1)} %get-tuple-element.119), channel_id=1, source_target_pairs={{0,4},{4,0},{8,12},{12,8},{16,20},{20,16},{24,28},{28,24},{1,5},{5... | collective-permute-start | bytes 2162696 | tf_op jit(solution)/shard_map/ppermute | solution.py:19
  666.4 46.2 %collective-permute-start.167 = (bf16[512,704]{0,1:T(8,128)(2,1)}, bf16[512,704]{0,1:T(8,128)(2,1)}, u32[]{:S(2)}, u32[]{:S(2)}) collective-permute-start(bf16[512,704]{0,1:T(8,128)(2,1)} %get-tuple-element.121), channel_id=1, source_target_pairs={{0,4},{4,0},{8,12},{12,8},{16,20},{20,16},{24,28},{28,24},{1,5},{5... | collective-permute-start | bytes 2162696 | tf_op jit(solution)/shard_map/ppermute | solution.py:19
  699.0 125.5 %collective-permute-start.86 = (bf16[512,1024]{1,0:T(8,128)(2,1)}, bf16[512,1024]{1,0:T(8,128)(2,1)}, u32[]{:S(2)}, u32[]{:S(2)}) collective-permute-start(bf16[512,1024]{1,0:T(8,128)(2,1)} %get-tuple-element.281), channel_id=1, source_target_pairs={{1,2},{2,1},{5,6},{6,5},{9,10},{10,9},{13,14},{14,13},{17,18},{18,... | collective-permute-start | bytes 3145736 | tf_op jit(solution)/shard_map/ppermute | solution.py:23
  708.9 46.0 %collective-permute-start.163 = (bf16[3,2,128,704]{2,3,0,1:T(8,128)(2,1)}, bf16[3,2,128,704]{2,3,0,1:T(8,128)(2,1)}, u32[]{:S(2)}, u32[]{:S(2)}) collective-permute-start(bf16[3,2,128,704]{2,3,0,1:T(8,128)(2,1)} %pad_maximum_fusion.8), channel_id=1, source_target_pairs={{0,8},{4,12},{8,0},{12,4},{16,24},{20,28},{24,16},{28,20},{1,9},{5... | collective-permute-start | bytes 3244040 | tf_op jit(solution)/shard_map/ppermute | solution.py:19
  712.5 75.2 %collective-permute-start.104 = (bf16[512,1024]{1,0:T(8,128)(2,1)}, bf16[512,1024]{1,0:T(8,128)(2,1)}, u32[]{:S(2)}, u32[]{:S(2)}) collective-permute-start(bf16[512,1024]{1,0:T(8,128)(2,1)} %get-tuple-element.93), channel_id=1, source_target_pairs={{0,1},{1,0},{2,3},{3,2},{4,5},{5,4},{6,7},{7,6},{8,9},{9,8},{10,11... | collective-permute-start | bytes 3145736 | tf_op jit(solution)/shard_map/ppermute | solution.py:23
  759.3 71.5 %collective-permute-start.106 = (bf16[512,1024]{1,0:T(8,128)(2,1)}, bf16[512,1024]{1,0:T(8,128)(2,1)S(1)}, u32[]{:S(2)}, u32[]{:S(2)}) collective-permute-start(bf16[512,1024]{1,0:T(8,128)(2,1)} %get-tuple-element.93), channel_id=1, source_target_pairs={{1,2},{2,1},{5,6},{6,5},{9,10},{10,9},{13,14},{14,13},{17,18},{18,... | collective-permute-start | bytes 3145736 | tf_op jit(solution)/shard_map/ppermute | solution.py:23
  785.9 41.5 %collective-permute-start.168 = (bf16[3,2,128,704]{2,3,0,1:T(8,128)(2,1)S(1)}, bf16[3,2,128,704]{2,3,0,1:T(8,128)(2,1)S(1)}, u32[]{:S(2)}, u32[]{:S(2)}) collective-permute-start(bf16[3,2,128,704]{2,3,0,1:T(8,128)(2,1)S(1)} %pad_maximum_fusion.9), channel_id=1, source_target_pairs={{0,8},{4,12},{8,0},{12,4},{16,24},{20,28},{24,16},{28,20},{1,9},{5... | collective-permute-start | bytes 3244040 | tf_op jit(solution)/shard_map/ppermute | solution.py:19
  839.1 45.2 %collective-permute-start.107 = (bf16[512,1024]{1,0:T(8,128)(2,1)S(1)}, bf16[512,1024]{1,0:T(8,128)(2,1)S(1)}, u32[]{:S(2)}, u32[]{:S(2)}) collective-permute-start(bf16[512,1024]{1,0:T(8,128)(2,1)S(1)} %collective-permute-done.106), channel_id=1, source_target_pairs={{2,3},{1,0},{6,7},{5,4},{10,11},{9,8},{14,15},{13,12},{18,19},{17,... | collective-permute-start | bytes 3145736 | tf_op jit(solution)/shard_map/ppermute | solution.py:23
  890.0 47.0 %collective-permute-start.108 = (bf16[512,1024]{1,0:T(8,128)(2,1)}, bf16[512,1024]{1,0:T(8,128)(2,1)}, u32[]{:S(2)}, u32[]{:S(2)}) collective-permute-start(bf16[512,1024]{1,0:T(8,128)(2,1)} %collective-permute-done.105), channel_id=1, source_target_pairs={{2,3},{1,0},{6,7},{5,4},{10,11},{9,8},{14,15},{13,12},{18,19},{17,... | collective-permute-start | bytes 3145736 | tf_op jit(solution)/shard_map/ppermute | solution.py:23
  896.6 43.1 %collective-permute-start.159 = (bf16[3,128,704]{1,2,0:T(8,128)(2,1)}, bf16[3,128,704]{1,2,0:T(8,128)(2,1)S(1)}, u32[]{:S(2)}, u32[]{:S(2)}) collective-permute-start(bf16[3,128,704]{1,2,0:T(8,128)(2,1)} %slice_bitcast_fusion.40), channel_id=1, source_target_pairs={{0,16},{4,20},{8,24},{12,28},{16,0},{20,4},{24,8},{28,12},{1,17},{... | collective-permute-start | bytes 1622024 | tf_op jit(solution)/shard_map/ppermute | solution.py:19
  900.8 38.9 %collective-permute-start.179 = (bf16[3,128,704]{1,2,0:T(8,128)(2,1)S(1)}, bf16[3,128,704]{1,2,0:T(8,128)(2,1)S(1)}, u32[]{:S(2)}, u32[]{:S(2)}) collective-permute-start(bf16[3,128,704]{1,2,0:T(8,128)(2,1)S(1)} %add_convert_fusion.11), channel_id=1, source_target_pairs={{1,2},{2,1},{5,6},{6,5},{9,10},{10,9},{13,14},{14,13},{17,18},{18,... | collective-permute-start | bytes 1622024 | tf_op jit(solution)/shard_map/ppermute | solution.py:23
  902.9 39.8 %collective-permute-start.177 = (bf16[3,128,704]{1,2,0:T(8,128)(2,1)S(1)}, bf16[3,128,704]{1,2,0:T(8,128)(2,1)S(1)}, u32[]{:S(2)}, u32[]{:S(2)}) collective-permute-start(bf16[3,128,704]{1,2,0:T(8,128)(2,1)S(1)} %get-tuple-element.83), channel_id=1, source_target_pairs={{2,3},{1,0},{6,7},{5,4},{10,11},{9,8},{14,15},{13,12},{18,19},{17,... | collective-permute-start | bytes 1622024 | tf_op jit(solution)/shard_map/ppermute | solution.py:23
  (455 other events, 4565.1 us)

commit v2 on v1

--- a/solution.py
+++ b/solution.py
@@ -1,6 +1,10 @@
+import functools
+
 import jax
 import jax.numpy as jnp
 from jax import lax
+from jax.experimental import pallas as pl
+from jax.experimental.pallas import tpu as pltpu
 from jax.sharding import PartitionSpec as P
 
 DH = 128
@@ -209,7 +213,7 @@
     return lax.dot_general(a, b, (((1,), (1,)), ((), ())), preferred_element_type=F32)
 
 
-def local(
+def local_plain(
     inputs,
     lengths,
     decays,
@@ -434,6 +438,730 @@
     )
 
 
+ROWS = 16
+BLOCK = 128
+SCALE = DH ** (-0.5)
+
+
+def shift_sum(source, taps, first, rows, step):
+    total = taps[0:1] * source[pl.ds(first, rows)]
+    for lag in range(1, KW):
+        total = total + taps[lag : lag + 1] * source[pl.ds(first + step * lag, rows)]
+    return total
+
+
+def live_rows(first, rows, length, segment_start):
+    place = segment_start + first + lax.broadcasted_iota(jnp.int32, (rows, 1), 0)
+    return (place < length).astype(F32)
+
+
+def live_columns(columns, length, segment_start):
+    return segment_start + lax.broadcasted_iota(jnp.int32, (1, columns), 1) < length
+
+
+def masked_scores(query, keys, pers_k, index, columns_live):
+    width = keys.shape[0]
+    raw = dot_t(query, keys) * SCALE
+    row = index * BLOCK + lax.broadcasted_iota(jnp.int32, (BLOCK, width), 0)
+    column = lax.broadcasted_iota(jnp.int32, (BLOCK, width), 1)
+    keep = (column <= row) & columns_live[:, :width]
+    return jnp.where(keep, raw, -1e30), dot_t(query, pers_k) * SCALE
+
+
+def forward_slot(k, refs, length, segment_start):
+    h_long, weights, taps, pers_k, pers_v, pre, zgate, query, keyed, valued, att, lse, write, wide = refs
+    seg = query.shape[1]
+    heads = query.shape[2] // DH
+    for i in range(3):
+        rounded = dot(h_long[...], weights[k, i]).astype(BF)
+        pre[i, k] = rounded
+        wide[i] = rounded.astype(F32)
+    zgate[k] = dot(h_long[pl.ds(ROWS, seg)], weights[k, 3])
+    for first in range(0, seg, BLOCK):
+        rows = pl.ds(first, BLOCK)
+        for i in range(3):
+            conv = shift_sum(wide.at[i], taps[k, i].astype(F32), ROWS + first, BLOCK, -1)
+            act = conv * jax.nn.sigmoid(conv)
+            if i == 2:
+                valued[k, rows] = act.astype(BF)
+                continue
+            target = (query, keyed)[i]
+            for head in range(heads):
+                lanes = slice(head * DH, (head + 1) * DH)
+                target[k, rows, lanes] = norm_keep(act[:, lanes])[0].astype(BF)
+    seg_live = live_rows(0, seg, length, segment_start).astype(BF)
+    columns_live = live_columns(seg, length, segment_start)
+    for head in range(heads):
+        lanes = slice(head * DH, (head + 1) * DH)
+        masked = valued[k, :, lanes] * seg_live
+        write[k, head] = (
+            lax.dot_general(
+                masked, keyed[k, :, lanes], (((0,), (0,)), ((), ())), preferred_element_type=F32
+            )
+            / seg
+        ).astype(BF)
+        for index in range(seg // BLOCK):
+            rows = pl.ds(index * BLOCK, BLOCK)
+            upto = pl.ds(0, (index + 1) * BLOCK)
+            score, pers = masked_scores(
+                query[k, rows, lanes], keyed[k, upto, lanes], pers_k[k, :, lanes], index, columns_live
+            )
+            top = jnp.maximum(
+                jnp.max(score, axis=-1, keepdims=True), jnp.max(pers, axis=-1, keepdims=True)
+            )
+            score, pers = jnp.exp(score - top), jnp.exp(pers - top)
+            total = jnp.sum(score, axis=-1, keepdims=True) + jnp.sum(pers, axis=-1, keepdims=True)
+            inverse = 1.0 / total
+            lse[k, head, rows] = top + jnp.log(total)
+            att[k, rows, lanes] = dot((score * inverse).astype(BF), valued[k, upto, lanes]) + dot(
+                (pers * inverse).astype(BF), pers_v[k, :, lanes]
+            )
+
+
+def forward_kernel(
+    place, x_long, gain, weights, taps, pers_k, pers_v,
+    h_long, pre, zgate, query, keyed, valued, att, lse, write, wide,
+):
+    for first in range(0, x_long.shape[0], 176):
+        rows = pl.ds(first, 176)
+        normed, _ = norm_keep(x_long[rows].astype(F32))
+        h_long[rows] = (normed * gain[...]).astype(BF)
+    refs = (h_long, weights, taps, pers_k, pers_v, pre, zgate, query, keyed, valued, att, lse, write, wide)
+
+    @pl.loop(0, 4)
+    def _(k):
+        forward_slot(k, refs, place[0], place[1])
+
+
+def read_slot(k, refs):
+    prior, query, zgate, att, readout, rinv, mixed = refs
+    seg = query.shape[1]
+    for head in range(query.shape[2] // DH):
+        lanes = slice(head * DH, (head + 1) * DH)
+        normed, inverse = norm_keep(dot_t(query[k, :, lanes], prior[k, head]))
+        readout[k, :, lanes] = normed
+        rinv[k, head] = inverse
+        mixed[k, :, lanes] = (
+            att[k, :, lanes] + jax.nn.sigmoid(zgate[k, :, lanes]) * normed
+        ).astype(BF)
+
+
+def mix_kernel(
+    place, x_long, cot, ffn_gain, prior, query, zgate, att, out_w,
+    h_two, gffn, mixed, middle, readout, rinv, acc,
+):
+    seg = cot.shape[0]
+    length, start = place[0], place[1]
+    refs = (prior, query, zgate, att, readout, rinv, mixed)
+
+    @pl.loop(0, 4)
+    def _(k):
+        read_slot(k, refs)
+        part = dot(mixed[k], out_w[k])
+
+        @pl.when(k == 0)
+        def _():
+            acc[...] = part
+
+        @pl.when(k > 0)
+        def _():
+            acc[...] += part
+
+    for first in range(0, seg, BLOCK):
+        rows = pl.ds(first, BLOCK)
+        live = live_rows(first, BLOCK, length, start)
+        value = x_long[pl.ds(ROWS + first, BLOCK)].astype(F32) + live * acc[rows]
+        middle[rows] = value
+        normed, _ = norm_keep(value)
+        h_two[rows] = (normed * ffn_gain[...]).astype(BF)
+        gffn[rows] = (live * cot[rows].astype(F32)).astype(BF)
+
+
+def ffn_kernel(h_two, gffn, gate_up, down, hidden, dgate, dup, out_acc, grad_acc):
+    @pl.when(pl.program_id(0) == 0)
+    def _():
+        out_acc[...] = jnp.zeros_like(out_acc)
+        grad_acc[...] = jnp.zeros_like(grad_acc)
+
+    gate_w, up_w, down_w = gate_up[0, 0], gate_up[0, 1], down[0]
+    rows_at_once = 256
+
+    @pl.loop(0, h_two.shape[0] // rows_at_once)
+    def _(part):
+        rows = pl.ds(pl.multiple_of(part * rows_at_once, rows_at_once), rows_at_once)
+        gate = dot(h_two[rows], gate_w)
+        up = dot(h_two[rows], up_w)
+        sigma = jax.nn.sigmoid(gate)
+        silu = gate * sigma
+        low = (silu * up).astype(BF)
+        hidden[0, rows] = low
+        out_acc[rows] += dot(low, down_w)
+        back = dot_t(gffn[rows], down_w)
+        low_gate = (back * up * (sigma * (1.0 + gate * (1.0 - sigma)))).astype(BF)
+        low_up = (back * silu).astype(BF)
+        dgate[0, rows] = low_gate
+        dup[0, rows] = low_up
+        grad_acc[rows] += dot_t(low_gate, gate_w) + dot_t(low_up, up_w)
+
+
+def tail_kernel(
+    place, cot, ffn_gain, query, zgate, out_w, middle, readout, rinv, out_acc, grad_acc,
+    output, dmiddle, gattn, datt, dzgate, dread, dprior, gain_grad,
+):
+    seg = cot.shape[0]
+    length, start = place[0], place[1]
+    gain_sum = jnp.zeros((1, cot.shape[1]), F32)
+    for first in range(0, seg, BLOCK):
+        rows = pl.ds(first, BLOCK)
+        live = live_rows(first, BLOCK, length, start)
+        value = middle[rows]
+        output[rows] = (value + live * out_acc[rows]).astype(BF)
+        normed, inverse = norm_keep(value)
+        grad = grad_acc[rows]
+        gain_sum = gain_sum + jnp.sum(grad * normed, axis=0, keepdims=True)
+        result = cot[rows].astype(F32) + norm_back(grad * ffn_gain[...], normed, inverse)
+        dmiddle[rows] = result
+        gattn[rows] = (live * result).astype(BF)
+    gain_grad[...] = gain_sum
+
+    @pl.loop(0, 4)
+    def _(k):
+        dmixed = dot_t(gattn[...], out_w[k])
+        datt[k] = dmixed.astype(BF)
+        sigma = jax.nn.sigmoid(zgate[k])
+        dzgate[k] = (dmixed * readout[k] * sigma * (1.0 - sigma)).astype(BF)
+        grad = dmixed * sigma
+        for head in range(dmixed.shape[1] // DH):
+            lanes = slice(head * DH, (head + 1) * DH)
+            low = norm_back(grad[:, lanes], readout[k, :, lanes], rinv[k, head]).astype(BF)
+            dread[k, :, lanes] = low
+            dprior[k, head] = lax.dot_general(
+                low, query[k, :, lanes], (((0,), (0,)), ((), ())), preferred_element_type=F32
+            ).astype(BF)
+
+
+def attention_back_slot(k, refs, length, segment_start):
+    query, keyed, valued, lse, datt, dread, prior, pers_k, pers_v, dqkv, dpers_k, dpers_v = refs
+    seg = query.shape[1]
+    columns_live = live_columns(seg, length, segment_start)
+    turn = lambda a, b: lax.dot_general(a, b, (((0,), (0,)), ((), ())), preferred_element_type=F32)
+    for head in range(query.shape[2] // DH):
+        lanes = slice(head * DH, (head + 1) * DH)
+        pers_keys_sum = jnp.zeros((pers_k.shape[1], DH), F32)
+        pers_values_sum = jnp.zeros((pers_k.shape[1], DH), F32)
+        dqkv[1, :, lanes] = jnp.zeros((seg, DH), F32)
+        dqkv[2, :, lanes] = jnp.zeros((seg, DH), F32)
+        dqkv[0, :, lanes] = dot(dread[k, :, lanes], prior[k, head])
+        for index in range(seg // BLOCK):
+            rows = pl.ds(index * BLOCK, BLOCK)
+            upto = pl.ds(0, (index + 1) * BLOCK)
+            q, d = query[k, rows, lanes], datt[k, rows, lanes]
+            keys, pk = keyed[k, upto, lanes], pers_k[k, :, lanes]
+            score, pers = masked_scores(q, keys, pk, index, columns_live)
+            log_total = lse[k, head, rows]
+            prob, prob_p = jnp.exp(score - log_total), jnp.exp(pers - log_total)
+            grad = dot_t(d, valued[k, upto, lanes])
+            grad_p = dot_t(d, pers_v[k, :, lanes])
+            row_dot = jnp.sum(prob * grad, axis=-1, keepdims=True) + jnp.sum(
+                prob_p * grad_p, axis=-1, keepdims=True
+            )
+            dscore = (prob * (grad - row_dot)).astype(BF)
+            dscore_p = (prob_p * (grad_p - row_dot)).astype(BF)
+            dqkv[0, rows, lanes] += (dot(dscore, keys) + dot(dscore_p, pk)) * SCALE
+            dqkv[1, upto, lanes] += turn(dscore, q) * SCALE
+            dqkv[2, upto, lanes] += turn(prob.astype(BF), d)
+            pers_keys_sum = pers_keys_sum + turn(dscore_p, q)
+            pers_values_sum = pers_values_sum + turn(prob_p.astype(BF), d)
+        dpers_k[k, :, lanes] = pers_keys_sum * SCALE
+        dpers_v[k, :, lanes] = pers_values_sum
+
+
+def conv_back_slot(k, refs, length, segment_start):
+    pre, taps, keyed, valued, dwrite, dqkv, dconv, grad_conv, wide = refs
+    seg = keyed.shape[1]
+    heads = keyed.shape[2] // DH
+    for i in range(3):
+        wide[i] = pre[i, k].astype(F32)
+    sums = [[jnp.zeros((1, heads * DH), F32) for _ in range(KW)] for _ in range(3)]
+    for first in range(0, seg, BLOCK):
+        rows = pl.ds(first, BLOCK)
+        live = live_rows(first, BLOCK, length, segment_start)
+        for i in range(3):
+            conv = shift_sum(wide.at[i], taps[k, i].astype(F32), ROWS + first, BLOCK, -1)
+            sigma = jax.nn.sigmoid(conv)
+            act = conv * sigma
+            parts = []
+            for head in range(heads):
+                lanes = slice(head * DH, (head + 1) * DH)
+                grad = dqkv[i, rows, lanes]
+                if i == 1:
+                    masked = valued[k, rows, lanes] * live.astype(BF)
+                    grad = grad + dot(masked, dwrite[k, head]) / seg
+                if i == 2:
+                    grad = grad + live * dot_t(keyed[k, rows, lanes], dwrite[k, head]) / seg
+                else:
+                    grad = norm_back(grad, *norm_keep(act[:, lanes]))
+                parts.append(grad)
+            result = jnp.concatenate(parts, axis=1) * (sigma * (1.0 + conv * (1.0 - sigma)))
+            dconv[i, k, rows] = result
+            for lag in range(KW):
+                sums[i][lag] = sums[i][lag] + jnp.sum(
+                    result * wide[i, pl.ds(ROWS + first - lag, BLOCK)], axis=0, keepdims=True
+                )
+    for i in range(3):
+        for lag in range(KW):
+            grad_conv[k, i, lag : lag + 1] = sums[i][lag]
+
+
+def back_kernel(
+    place, query, keyed, valued, lse, datt, dread, prior, pers_k, pers_v, pre, taps, dwrite,
+    dconv, dpers_k, dpers_v, grad_conv, dqkv, wide,
+):
+    length, start = place[0], place[1]
+    one = (query, keyed, valued, lse, datt, dread, prior, pers_k, pers_v, dqkv, dpers_k, dpers_v)
+    two = (pre, taps, keyed, valued, dwrite, dqkv, dconv, grad_conv, wide)
+
+    @pl.loop(0, 4)
+    def _(k):
+        attention_back_slot(k, one, length, start)
+        conv_back_slot(k, two, length, start)
+
+
+def input_kernel(
+    x_long, gain, dconv, after, taps, weights, dzgate, dmiddle,
+    dpre, input_grad, gain_grad, longer, acc,
+):
+    seg = dmiddle.shape[0]
+    acc[...] = jnp.zeros_like(acc)
+
+    @pl.loop(0, 4)
+    def _(k):
+        for i in range(3):
+            longer[pl.ds(0, seg)] = dconv[i, k]
+            longer[pl.ds(seg, 8)] = after[i, k]
+            for first in range(0, seg, BLOCK):
+                dpre[i, k, pl.ds(first, BLOCK)] = shift_sum(
+                    longer, taps[k, i].astype(F32), first, BLOCK, 1
+                ).astype(BF)
+        total = dot_t(dpre[0, k], weights[k, 0])
+        for i in (1, 2):
+            total = total + dot_t(dpre[i, k], weights[k, i])
+        acc[...] += total + dot_t(dzgate[k], weights[k, 3])
+
+    gain_sum = jnp.zeros((1, acc.shape[1]), F32)
+    for first in range(0, seg, BLOCK):
+        rows = pl.ds(first, BLOCK)
+        normed, inverse = norm_keep(x_long[pl.ds(ROWS + first, BLOCK)].astype(F32))
+        grad = acc[rows]
+        gain_sum = gain_sum + jnp.sum(grad * normed, axis=0, keepdims=True)
+        input_grad[rows] = (
+            dmiddle[rows] + norm_back(grad * gain[...], normed, inverse)
+        ).astype(BF)
+    gain_grad[...] = gain_sum
+
+
+SHAPE = jax.ShapeDtypeStruct
+VMEM_LIMIT = 60 * 1024 * 1024
+
+
+def call(kernel, outs, scratch, smem, *args):
+    specs = [pl.BlockSpec(memory_space=pltpu.SMEM)] * smem
+    specs += [pl.BlockSpec(memory_space=pltpu.VMEM)] * (len(args) - smem)
+    return pl.pallas_call(
+        kernel,
+        out_shape=outs,
+        in_specs=specs,
+        out_specs=[pl.BlockSpec(memory_space=pltpu.VMEM)] * len(outs),
+        scratch_shapes=scratch,
+        compiler_params=pltpu.CompilerParams(vmem_limit_bytes=VMEM_LIMIT),
+    )(*args)
+
+
+MESH = pl.DeviceIdType.MESH
+SKEW_ONE, SKEW_TWO = 2, 4
+
+
+class Links:
+    def __init__(self, send, recv):
+        self.send, self.recv = send, recv
+        self.sent = 0
+        self.names = {}
+        self.always, self.middles = [], []
+        self.p, self.z = lax.axis_index("seq"), lax.axis_index("head")
+        self.middle = (self.z == 1) | (self.z == 2)
+
+    def greet(self):
+        barrier = pltpu.get_barrier_semaphore()
+        for flip in (1, 2, 4):
+            pl.semaphore_signal(barrier, device_id=(self.p ^ flip, self.z), device_id_type=MESH)
+        for flip in (1, 3):
+            pl.semaphore_signal(barrier, device_id=(self.p, self.z ^ flip), device_id_type=MESH)
+        pl.semaphore_wait(barrier, 5)
+
+    def place(self, name):
+        return self.recv.at[self.names.setdefault(name, len(self.names))]
+
+    def copy(self, source, target, name, device):
+        index = self.sent
+        self.sent += 1
+        return pltpu.make_async_remote_copy(
+            src_ref=source, dst_ref=target, send_sem=self.send.at[index], recv_sem=self.place(name),
+            device_id=device, device_id_type=MESH,
+        )
+
+    def along_seq(self, source, target, name, flip):
+        copy = self.copy(source, target, name, (self.p ^ flip, self.z))
+        copy.start()
+        self.always.append((lambda: source, self.sent - 1))
+
+    def along_head(self, source, target, name, flip, waits):
+        index = self.sent
+        copy = self.copy(source(), target(), name, (self.p, self.z ^ flip))
+        copy.start()
+        waits.append((source, index))
+
+    def arrived(self, target, name):
+        pltpu.make_async_remote_copy(
+            src_ref=target, dst_ref=target, send_sem=self.send.at[0], recv_sem=self.place(name),
+            device_id=(self.p, self.z ^ 1), device_id_type=MESH,
+        ).wait_recv()
+
+    def gone(self, source, index):
+        pltpu.make_async_remote_copy(
+            src_ref=source(), dst_ref=source(), send_sem=self.send.at[index], recv_sem=self.recv.at[0],
+            device_id=(self.p, self.z ^ 1), device_id_type=MESH,
+        ).wait_send()
+
+    def finish(self):
+        for source, index in self.always:
+            self.gone(source, index)
+
+        @pl.when(self.middle)
+        def _():
+            for source, index in self.middles:
+                self.gone(source, index)
+
+
+class LineGather:
+    def __init__(self, links, name, view):
+        self.links, self.name, self.view = links, name, view
+
+    def start(self, sources):
+        links = self.links
+        for source, view in sources:
+            links.along_head(source, lambda: view(1), (self.name, 1), 1, links.always)
+
+        @pl.when(links.middle)
+        def _():
+            for source, view in sources:
+                links.along_head(source, lambda: view(3), (self.name, 3), 3, links.middles)
+
+    def step(self, k):
+        links, name, view = self.links, self.name, self.view
+        if k == 1:
+            links.arrived(view(1), (name, 1))
+
+            @pl.when(links.middle)
+            def _():
+                links.along_head(lambda: view(1), lambda: view(2), (name, 2), 3, links.middles)
+                links.arrived(view(3), (name, 3))
+                links.along_head(lambda: view(3), lambda: view(2), (name, 2), 1, links.middles)
+
+        if k == 2:
+            links.arrived(view(2), (name, 2))
+
+            @pl.when(links.middle)
+            def _():
+                links.along_head(lambda: view(2), lambda: view(3), (name, 3), 1, links.middles)
+
+        if k == 3:
+
+            @pl.when(~links.middle)
+            def _():
+                links.arrived(view(3), (name, 3))
+
+
+class PlaneGather:
+    def __init__(self, links, name, view, x_first):
+        self.links, self.name, self.view = links, name, view
+        self.near, self.far = (2, 4) if x_first else (4, 2)
+
+    def send(self, j, flip):
+        links = self.links
+        block = self.view(links.p ^ j)
+        links.along_seq(block, block, (self.name, j ^ flip), flip)
+
+    def wait(self, j):
+        self.links.arrived(self.view(self.links.p ^ j), (self.name, j))
+
+    def start(self):
+        self.send(0, self.near)
+        self.send(0, self.far)
+        self.send(0, 1)
+
+    def step(self):
+        self.wait(self.near)
+        self.send(self.near, self.far)
+        self.send(self.near, 1)
+        self.wait(self.far)
+        self.send(self.far, 1)
+
+    def last(self):
+        self.wait(6)
+        self.send(6, 1)
+
+    def end(self):
+        for j in (1, 3, 5, 7):
+            self.wait(j)
+
+
+def weight_pieces(links, weights, out_w, gate_up, down):
+    block = lambda q: pl.ds(pl.multiple_of(q * 128, 128), 128)
+    views = {
+        "proj": (lambda k, q: weights.at[k, :, block(q), :], True),
+        "out": (lambda k, q: out_w.at[k, :, block(q)], False),
+        "ffn": (lambda k, q: gate_up.at[k, :, block(q), :], False),
+        "down": (lambda k, q: down.at[k, :, block(q)], True),
+    }
+    pieces = {}
+    for name, (view, x_first) in views.items():
+        line = LineGather(links, name, lambda k, view=view: view(k, links.p))
+        planes = [
+            PlaneGather(links, (name, k), lambda q, view=view, k=k: view(k, q), x_first)
+            for k in (1, 2, 3)
+        ]
+        pieces[name] = (line, planes)
+    return pieces
+
+
+def weight_events(links, own, weights, out_w, gate_up, down):
+    q_own, k_own, v_own, g_own, o_own, gate_own, up_own, down_own = own
+    mine = pl.ds(pl.multiple_of(links.p * 128, 128), 128)
+    pieces = weight_pieces(links, weights, out_w, gate_up, down)
+    starts = {
+        "proj": [
+            (lambda ref=ref: ref.at[mine, :], lambda k, i=i: weights.at[k, i, mine, :])
+            for i, ref in enumerate((q_own, k_own, v_own, g_own))
+        ],
+        "out": [(lambda: o_own.at[:, mine], lambda k: out_w.at[k, :, mine])],
+        "ffn": [
+            (lambda ref=ref: ref.at[mine, :], lambda k, i=i: gate_up.at[k, i, mine, :])
+            for i, ref in enumerate((gate_own, up_own))
+        ],
+        "down": [(lambda: down_own.at[:, mine], lambda k: down.at[k, :, mine])],
+    }
+    begin = lambda name: pieces[name][0].start(starts[name])
+    units = [("proj", k) for k in (1, 2, 3)] + [("out", k) for k in (1, 2, 3)]
+    units += [(name, k) for k in (1, 2, 3) for name in ("ffn", "down")]
+    when = {0: ["proj"], 1: ["out"], 2: ["ffn"], 3: ["down"]}
+    count = len(units)
+    events = []
+    for i in range(count + SKEW_TWO):
+        for name in when.get(i, []):
+            events.append((None, lambda name=name: begin(name)))
+        if i < count:
+            name, k = units[i]
+
+            def first(name=name, k=k):
+                pieces[name][0].step(k)
+                pieces[name][1][k - 1].start()
+
+            events.append((None, first))
+        if 0 <= i - SKEW_ONE < count:
+            name, k = units[i - SKEW_ONE]
+            events.append((None, pieces[name][1][k - 1].step))
+        if 0 <= i - SKEW_TWO < count:
+            name, k = units[i - SKEW_TWO]
+            events.append(((name, k), pieces[name][1][k - 1].last))
+    return events, pieces
+
+
+def gather_kernel(
+    q_own, k_own, v_own, g_own, o_own, gate_own, up_own, down_own,
+    weights, out_w, gate_up, down, send, recv,
+):
+    links = Links(send, recv)
+    links.greet()
+    own = (q_own, k_own, v_own, g_own, o_own, gate_own, up_own, down_own)
+    events, pieces = weight_events(links, own, weights, out_w, gate_up, down)
+    for _, step in events:
+        step()
+    for line, planes in pieces.values():
+        for plane in planes:
+            plane.end()
+    links.finish()
+
+
+def gather_all(own):
+    features, width = own[0].shape
+    hidden_width = own[5].shape[1]
+    anywhere = pl.BlockSpec(memory_space=pl.ANY)
+    low = lambda *shape: jax.ShapeDtypeStruct(shape, BF)
+    return pl.pallas_call(
+        gather_kernel,
+        out_shape=[
+            low(4, 4, features, width), low(4, width, features), low(4, 2, features, hidden_width),
+            low(4, hidden_width, features),
+        ],
+        in_specs=[anywhere] * 8,
+        out_specs=[anywhere] * 4,
+        scratch_shapes=[
+            pltpu.SemaphoreType.DMA((128,)), pltpu.SemaphoreType.DMA((128,)),
+        ],
+        compiler_params=pltpu.CompilerParams(collective_id=0, has_side_effects=True),
+    )(*own)
+
+
+def local_fast(
+    inputs, lengths, decays, norm_gain, query_proj, key_proj, value_proj, gate_proj, conv_taps,
+    pers_keys, pers_values, out_proj, ffn_gain, ffn_gate, ffn_up, ffn_down, cotangent,
+):
+    seqs, seg, features = inputs.shape
+    segments, shards = lax.axis_size("seq"), lax.axis_size("head")
+    p, z = lax.axis_index("seq"), lax.axis_index("head")
+    width, hidden_width = query_proj.shape[1], ffn_gate.shape[1]
+    heads_here = width // DH
+    heads = heads_here * shards
+    persistent = pers_keys.shape[0]
+
+    weights, out_w, gate_up, down_w = gather_all(
+        (query_proj, key_proj, value_proj, gate_proj, out_proj, ffn_gate, ffn_up, ffn_down)
+    )
+    weights = weights.at[0].set(jnp.stack([query_proj, key_proj, value_proj, gate_proj]))
+    out_w = out_w.at[0].set(out_proj)
+    gate_up = gate_up.at[0].set(jnp.stack([ffn_gate, ffn_up]))
+    down_w = down_w.at[0].set(ffn_down)
+    small = jnp.stack(
+        gather_small(jnp.concatenate([conv_taps.reshape(3 * KW, width), pers_keys, pers_values]))
+    )
+    taps = small[:, : 3 * KW].reshape(shards, 3, KW, width)
+    pers_k = small[:, 3 * KW : 3 * KW + persistent]
+    pers_v = small[:, 3 * KW + persistent :]
+
+    mine = lax.dynamic_index_in_dim(decays, z, 1, False)[:, 0]
+    mine = jnp.concatenate(
+        [lax.dynamic_slice_in_dim(mine, slot_owner(k) * heads_here, heads_here, 1) for k in range(shards)],
+        axis=1,
+    )
+    every = lax.all_gather(mine, "seq")
+    carry = carry_coefficients(every[:, 0], every[:, 1])
+
+    x = lax.dynamic_index_in_dim(inputs, z, 0, False)
+    cot = lax.dynamic_index_in_dim(cotangent, z, 0, False)
+    length = lax.dynamic_index_in_dim(lengths, z, 0, False)
+    place = jnp.stack([length, p * seg]).astype(jnp.int32)
+    before = lax.ppermute(x[seg - ROWS :], "seq", [(i, i + 1) for i in range(segments - 1)])
+    x_long = jnp.concatenate([before, x])
+    gain = norm_gain[None]
+    ffn_gain = ffn_gain[None]
+    low = lambda *shape: SHAPE(shape, BF)
+    full = lambda *shape: SHAPE(shape, F32)
+    rows_low = low(shards, seg, width)
+    rows_full = full(shards, seg, width)
+    state = low(shards, heads_here, DH, DH)
+    wide = pltpu.VMEM((3, seg + ROWS, width), F32)
+
+    h_long, pre, zgate, query, keyed, valued, att, lse, write = call(
+        forward_kernel,
+        [
+            low(seg + ROWS, features), low(3, shards, seg + ROWS, width), rows_full,
+            rows_low, rows_low, rows_low, rows_full, full(shards, heads_here, seg, 1), state,
+        ],
+        [wide],
+        1,
+        place, x_long, gain, weights, taps, pers_k, pers_v,
+    )
+
+    def mix_states(values, coefficients):
+        pieces, places = gather_states(values)
+        total = 0.0
+        coefficients = coefficients.reshape(segments, shards, heads_here)
+        for piece, at in zip(pieces, places):
+            coefficient = lax.dynamic_index_in_dim(coefficients, at, 0, False)
+            total = total + coefficient[:, :, None, None] * piece.astype(F32)
+        return total.astype(BF)
+
+    prior = mix_states(write, lax.dynamic_index_in_dim(carry, p, 0, False))
+    h_two, gffn, mixed, middle, readout, rinv = call(
+        mix_kernel,
+        [
+            low(seg, features), low(seg, features), rows_low, full(seg, features), rows_full,
+            full(shards, heads_here, seg, 1),
+        ],
+        [pltpu.VMEM((seg, features), F32)],
+        1,
+        place, x_long, cot, ffn_gain, prior, query, zgate, att, out_w,
+    )
+    hid = low(shards, seg, hidden_width)
+    whole = pl.BlockSpec((seg, features), lambda k: (0, 0))
+    part = pl.BlockSpec((1, seg, hidden_width), lambda k: (k, 0, 0))
+    hidden, dgate, dup, out_acc, grad_acc = pl.pallas_call(
+        ffn_kernel,
+        grid=(shards,),
+        out_shape=[hid, hid, hid, full(seg, features), full(seg, features)],
+        in_specs=[
+            whole, whole,
+            pl.BlockSpec((1, 2, features, hidden_width), lambda k: (k, 0, 0, 0)),
+            pl.BlockSpec((1, hidden_width, features), lambda k: (k, 0, 0)),
+        ],
+        out_specs=[part, part, part, whole, whole],
+        compiler_params=pltpu.CompilerParams(vmem_limit_bytes=VMEM_LIMIT),
+    )(h_two, gffn, gate_up, down_w)
+    output, dmiddle, gattn, datt, dzgate, dread, dprior, g_ffn_gain = call(
+        tail_kernel,
+        [
+            low(seg, features), full(seg, features), low(seg, features), rows_low, rows_low, rows_low,
+            state, full(1, features),
+        ],
+        [],
+        1,
+        place, cot, ffn_gain, query, zgate, out_w, middle, readout, rinv, out_acc, grad_acc,
+    )
+    output = gather_rows(output)
+    split = lambda value: [value[k] for k in range(shards)]
+    g_gate, g_up, g_down = weight_grads(
+        [(h_two, split(dgate)), (h_two, split(dup)), (gffn, split(hidden))], True
+    )
+    dwrite = mix_states(dprior, lax.dynamic_index_in_dim(carry, p, 1, False))
+    dconv, dpers_k, dpers_v, grad_conv = call(
+        back_kernel,
+        [
+            full(3, shards, seg, width), full(shards, persistent, width), full(shards, persistent, width),
+            full(shards, 3, KW, width),
+        ],
+        [pltpu.VMEM((3, seg, width), F32), wide],
+        1,
+        place, query, keyed, valued, lse, datt, dread, prior, pers_k, pers_v, pre, taps, dwrite,
+    )
+    after = lax.ppermute(dconv[:, :, :8], "seq", [(i + 1, i) for i in range(segments - 1)])
+    dpre, input_grad, g_norm_gain = call(
+        input_kernel,
+        [low(3, shards, seg, width), low(seg, features), full(1, features)],
+        [pltpu.VMEM((seg + 8, width), F32), pltpu.VMEM((seg, features), F32)],
+        0,
+        x_long, gain, dconv, after, taps, weights, dzgate, dmiddle,
+    )
+    input_grad = gather_rows(input_grad)
+    h_one = h_long[ROWS:]
+    g_query, g_key, g_value, g_zgate, g_out = weight_grads(
+        [(h_one, split(d)) for d in (dpre[0], dpre[1], dpre[2], dzgate)] + [(gattn, split(mixed))],
+        False,
+    )
+    rows = jnp.concatenate([grad_conv.reshape(shards, 3 * KW, width), dpers_k, dpers_v], axis=1)
+    gains = jnp.concatenate([g_norm_gain, g_ffn_gain]).reshape(-1, width)
+    rows, gains = sum_small(split(rows), gains)
+    gains = gains.reshape(2, features)
+    return (
+        output, input_grad, gains[0], g_query, g_key, g_value, g_zgate,
+        rows[: 3 * KW].reshape(3, KW, width), rows[3 * KW : 3 * KW + persistent], rows[3 * KW + persistent :],
+        g_out.T, gains[1], g_gate, g_up, g_down.T,
+    )
+
+
+def local(*args):
+    return local_fast(*args) if custom_mesh() else local_plain(*args)
+
+
 def solution(mesh):
     in_specs = (
         P(None, "seq", None),

time: 953 us -> 809 us (0.85)
  Pallas kernels: 0 us -> 251 us
  matrix products: 223 us -> 75.4 us
  local copies, waits for them, and re-layouts: 217 us -> 139 us
  other arithmetic: 110 us -> 33.5 us
  starting transfers between devices: 167 us -> 112 us
  waiting for transfers between devices: 212 us -> 175 us
    pallas_call x0 -> x7, Pallas kernels: none -> 251 us  [the longest x1 115 us: gather_all(): pl.pallas_call(gather_kernel, out_shape=[low(4, 4, features, width), low(...]
    dot_general x46 -> x0, matrix products: 126 us -> none  [the longest x17 47 us: dot_t(): lax.dot_general(a, b, (((1,), (1,)), ((), ())), preferred_element_type=F32)]
    ppermute x139 -> x83, starting transfers between devices: 83 us -> 39.4 us  [along_seq(): return lax.ppermute(value, 'seq', [(i, i ^ flip) for i in range(8)])]
    dynamic_update_slice x36 -> x0, local copies, waits for them, and re-layouts: 39.6 us -> none  [gather_weights(): full = lax.dynamic_update_slice_in_dim(full, part, (p ^ j) * block, 1)]
    ppermute x40 -> x30, waiting for transfers between devices: 78.5 us -> 44.5 us  [along_head(): return lax.ppermute(value, 'head', pairs)]
    squeeze x5 -> x21, local copies, waits for them, and re-layouts: 9.43 us -> 38.4 us  [the longest x19 34.8 us: local_fast(): split = lambda value: [value[k] for k in range(shards)]]
    unnamed x656 -> x257, local copies, waits for them, and re-layouts: 53 us -> 27.8 us
    reduce_sum x6 -> x0, other arithmetic: 23.8 us -> none  [the longest x1 15.2 us: local(): jnp.sum(dconv * wide_pre[:, HALO - lag:HALO - lag + seg], axis=1)]
  transfers between devices with their start and end apart: 181 -> 115, of which waited for: 38 -> 28; matrix products, arithmetic and copies ran while one was open for 54% -> 28% of each run, Pallas kernels for 0% -> 28%
where the time goes in v2:
time: 809 us; the launch traced here: 798 us
  Pallas kernels  251 us (31%)
  waiting for transfers between devices  175 us (22%)
  local copies, waits for them, and re-layouts  139 us (17%)
  starting transfers between devices  112 us (14%)
  matrix products  75.4 us (9%)
  other arithmetic  33.5 us (4%)
  blocking collectives  9.18 us (1%)
    ppermute x83, waiting for transfers between devices, along_seq(): return lax.ppermute(value, 'seq', [(i, i ^ flip) for i in range(8)])  129 us
    pallas_call x1, Pallas kernels, gather_all(): pl.pallas_call(gather_kernel, out_shape=[low(4, 4, features, width), low(...  115 us
    pallas_call x5, Pallas kernels, call(): pl.pallas_call(kernel, out_shape=outs, in_specs=specs, out_specs=[pl.Bloc...  101 us
    dot_general x64, matrix products, weight_grads(): lax.dot_general(a, b, (((0,), (0,)), ((), ())), preferred_element_type=F32)  75.4 us
    ppermute x30, starting transfers between devices, along_head(): return lax.ppermute(value, 'head', pairs)  69 us
    ppermute x30, waiting for transfers between devices, along_head(): return lax.ppermute(value, 'head', pairs)  44.5 us
    ppermute x83, starting transfers between devices, along_seq(): return lax.ppermute(value, 'seq', [(i, i ^ flip) for i in range(8)])  39.4 us
    squeeze x19, local copies, waits for them, and re-layouts, local_fast(): split = lambda value: [value[k] for k in range(shards)]  34.8 us
  transfers between devices with their start and end apart: 115, of which 28 were waited for; matrix products, arithmetic and copies ran while one was open for 28% of the time, Pallas kernels for 28%

profile of v2, /device:TPU:0, one launch (start us, length us, event | category | flops | bytes accessed | tf_op | source)
XLA Modules:
  0.0 797.7 jit_solution(5134222464337551174)
XLA Ops:
  2.8 3.0 collective-permute-start.1
  13.3 9.2 %all-gather.1 = f32[8,2,8]{2,1,0:T(2,128)S(1)} all-gather(f32[1,2,8]{2,1,0:T(2,128)S(1)} %maximum_bitcast_fusion.2), channel_id=2, replica_groups=mesh['seq'=8,'head'=4] {'seq'}, dimensions={0}, use_global_device_ids=true | all-gather | bytes 576 | tf_op jit(solution)/shard_map/all_gather | solution.py:1046
  28.5 114.9 %shard_map.280 = (bf16[4,4,1024,256]{3,2,1,0:T(8,128)(2,1)}, bf16[4,256,1024]{2,1,0:T(8,128)(2,1)}, bf16[4,2,1024,704]{3,2,1,0:T(8,128)(2,1)}, bf16[4,704,1024]{2,1,0:T(8,128)(2,1)}) custom-call(bf16[1024,256]{1,0:T(8,128)(2,1)} %q_own.1, bf16[1024,256]{1,0:T(8,128)(2,1)} %k_own.1, bf16[1024,256]{1,0:T(8,128)(2,1)} %v_own.1, bf16[1024,256]{1,0:T(8,128)(2,1)} %g_own.1, ...), custom_call_target="tpu_custom_call" | custom-call | tf_op jit(solution)/shard_map/pallas_call | solution.py:1000
  160.0 28.9 %shard_map.281 = (bf16[528,1024]{1,0:T(8,128)(2,1)}, bf16[3,4,528,256]{3,2,1,0:T(8,128)(2,1)}, f32[4,512,256]{2,1,0:T(8,128)}, bf16[4,512,256]{2,1,0:T(8,128)(2,...) custom-call(s32[2]{0:T(128)} %pad_add_fusion.place, ...), custom_call_target="tpu_custom_call" | custom-call | tf_op jit(solution)/shard_map/pallas_call | solution.py:770
  196.5 2.9 collective-permute-done.11
  210.5 12.2 %shard_map.282 = (bf16[512,1024]{1,0:T(8,128)(2,1)}, bf16[512,1024]{1,0:T(8,128)(2,1)}, bf16[4,512,256]{2,1,0:T(8,128)(2,1)}, f32[512,1024]{1,0:T(8,128)}, f32[4...) custom-call(s32[2]{0:T(128)} %pad_add_fusion.place, bf16[528,1024]{1,0:T(8,128)(2,1)} %pad_maximum_fusion.x_long, ...), custom_call_target="tpu_custom_call" | custom-call | tf_op jit(solution)/shard_map/pallas_call | solution.py:770
  225.3 34.8 %shard_map.283 = (bf16[4,512,704]{2,1,0:T(8,128)(2,1)}, bf16[4,512,704]{2,1,0:T(8,128)(2,1)}, bf16[4,512,704]{2,1,0:T(8,128)(2,1)}, f32[512,1024]{1,0:T(8,128)}, f32[512,1024]{1,0:T(8,128)}) custom-call(bf16[512,1024]{1,0:T(8,128)(2,1)} %get-tuple-element.111.h_two, bf16[512,1024]{1,0:T(8,128)(2,1)} %get-tuple-element.112.gffn, ...), custom_call_target="tpu_custom_call" | custom-call | tf_op jit(solution)/shard_map/pallas_call | solution.py:1098
  260.1 3.4 slice_bitcast_fusion.10
  289.1 13.4 %shard_map.284 = (bf16[512,1024]{1,0:T(8,128)(2,1)}, f32[512,1024]{1,0:T(8,128)}, bf16[512,1024]{1,0:T(8,128)(2,1)}, bf16[4,512,256]{2,1,0:T(8,128)(2,1)}, bf16[...) custom-call(s32[2]{0:T(128)} %pad_add_fusion.place, ...), custom_call_target="tpu_custom_call" | custom-call | tf_op jit(solution)/shard_map/pallas_call | solution.py:770
  365.9 31.5 %shard_map.285 = (f32[3,4,512,256]{3,2,1,0:T(8,128)}, f32[4,16,256]{2,1,0:T(8,128)}, f32[4,16,256]{2,1,0:T(8,128)}, f32[4,3,4,256]{3,2,1,0:T(4,128)}) custom-call(s32[2]{0:T(128)} %pad_add_fusion.place, bf16[4,512,256]{2,1,0:T(8,128)(2,1)} %get-tuple-element.103.query, bf16[4,512,256]{2,1,0:T(8,128)(2,1)} %get-tuple-element.118.keyed, ...), custom_call_target="tpu_custom_call" | custom-call | tf_op jit(solution)/shard_map/pallas_call | solution.py:770
  411.7 15.3 %shard_map.286 = (bf16[3,4,512,256]{3,2,1,0:T(8,128)(2,1)}, bf16[512,1024]{1,0:T(8,128)(2,1)}, f32[1,1024]{1,0:T(1,128)}) custom-call(bf16[528,1024]{1,0:T(8,128)(2,1)} %pad_maximum_fusion.x_long, f32[1,1024]{1,0:T(1,128)} %bitcast.479, f32[3,4,512,256]{3,2,1,0:T(8,128)} %get-tuple-element.125.dconv, f32[3,4,8,256]{3,2,1,0:T(8,128)} %copy-done.104, ...), custom_call_target="tpu_custom_call" | custom-call | tf_op jit(solution)/shard_map/pallas_call | solution.py:770
  429.1 3.5 slice_bitcast_fusion.48
  482.4 3.0 fusion.13
  488.2 3.0 fusion.12
  493.6 3.0 fusion.11
  503.1 3.2 collective-permute-start.38
  513.1 3.0 fusion.85
  562.3 11.2 %collective-permute-done.58 = bf16[5,2,128,256]{3,2,0,1:T(8,128)(2,1)S(1)} collective-permute-done((bf16[5,2,128,256]{3,2,0,1:T(8,128)(2,1)S(1)}, bf16[5,2,128,256]{3,2,0,1:T(8,128)(2,1)S(1)}, u32[]{:S(2)}, u32[]{:S(2)}) %collective-permute-start.58) | collective-permute-done | bytes 655392 | tf_op jit(solution)/shard_map/ppermute | solution.py:23
  574.0 13.5 %collective-permute-done.72 = bf16[5,2,128,256]{3,2,0,1:T(8,128)(2,1)S(1)} collective-permute-done((bf16[5,2,128,256]{3,2,0,1:T(8,128)(2,1)S(1)}, bf16[5,2,128,256]{3,2,0,1:T(8,128)(2,1)S(1)}, u32[]{:S(2)}, u32[]{:S(2)}) %collective-permute-start.72) | collective-permute-done | bytes 655392 | tf_op jit(solution)/shard_map/ppermute | solution.py:23
  588.0 13.6 %collective-permute-done.79 = bf16[5,2,128,256]{3,2,0,1:T(8,128)(2,1)S(1)} collective-permute-done((bf16[5,2,128,256]{3,2,0,1:T(8,128)(2,1)S(1)}, bf16[5,2,128,256]{3,2,0,1:T(8,128)(2,1)S(1)}, u32[]{:S(2)}, u32[]{:S(2)}) %collective-permute-start.79) | collective-permute-done | bytes 655392 | tf_op jit(solution)/shard_map/ppermute | solution.py:23
  602.1 12.5 %collective-permute-done.65 = bf16[5,2,128,256]{3,2,0,1:T(8,128)(2,1)S(1)} collective-permute-done((bf16[5,2,128,256]{3,2,0,1:T(8,128)(2,1)S(1)}, bf16[5,2,128,256]{3,2,0,1:T(8,128)(2,1)S(1)}, u32[]{:S(2)}, u32[]{:S(2)}) %collective-permute-start.65) | collective-permute-done | bytes 655392 | tf_op jit(solution)/shard_map/ppermute | solution.py:23
  619.2 16.2 %collective-permute-done.80 = bf16[5,128,256]{2,1,0:T(8,128)(2,1)S(1)} collective-permute-done((bf16[5,128,256]{2,1,0:T(8,128)(2,1)S(1)}, bf16[5,128,256]{2,1,0:T(8,128)(2,1)S(1)}, u32[]{:S(2)}, u32[]{:S(2)}) %collective-permute-start.80) | collective-permute-done | bytes 327712 | tf_op jit(solution)/shard_map/ppermute | solution.py:23
  640.1 18.5 %collective-permute-done.107 = bf16[3,2,128,704]{2,3,0,1:T(8,128)(2,1)S(1)} collective-permute-done((bf16[3,2,128,704]{2,3,0,1:T(8,128)(2,1)S(1)}, bf16[3,2,128,704]{2,3,0,1:T(8,128)(2,1)S(1)}, u32[]{:S(2)}, u32[]{:S(2)}) %collective-permute-start.107) | collective-permute-done | bytes 1081376 | tf_op jit(solution)/shard_map/ppermute | solution.py:23
  659.1 22.6 %collective-permute-done.97 = bf16[3,2,128,704]{2,3,0,1:T(8,128)(2,1)S(1)} collective-permute-done((bf16[3,2,128,704]{2,3,0,1:T(8,128)(2,1)S(1)}, bf16[3,2,128,704]{2,3,0,1:T(8,128)(2,1)S(1)}, u32[]{:S(2)}, u32[]{:S(2)}) %collective-permute-start.97) | collective-permute-done | bytes 1081376 | tf_op jit(solution)/shard_map/ppermute | solution.py:23
  686.1 3.4 collective-permute-done.81
  689.7 4.4 collective-permute-start.84
  701.3 6.2 collective-permute-start.109
  714.9 19.7 %collective-permute-start.86 = (bf16[5,128,256]{2,1,0:T(8,128)(2,1)S(1)}, bf16[5,128,256]{2,1,0:T(8,128)(2,1)S(1)}, u32[]{:S(2)}, u32[]{:S(2)}) collective-permute-start(bf16[5,128,256]{2,1,0:T(8,128)(2,1)S(1)} %get-tuple-element.176), channel_id=1, source_target_pairs={{0,1},{3,2},{4,5},{7,6},{8,9},{11,10},{12,13},{15,14},{16,17},{19,... | collective-permute-start | bytes 983048 | tf_op jit(solution)/shard_map/ppermute | solution.py:27
  746.0 2.7 collective-permute-done.112
  755.4 13.1 %collective-permute-done.22 = bf16[512,1024]{1,0:T(8,128)(2,1)} collective-permute-done((bf16[512,1024]{1,0:T(8,128)(2,1)}, bf16[512,1024]{1,0:T(8,128)(2,1)}, u32[]{:S(2)}, u32[]{:S(2)}) %collective-permute-start.22) | collective-permute-done | bytes 1048608 | tf_op jit(solution)/shard_map/ppermute | solution.py:27
  772.7 17.7 %collective-permute-done.42 = bf16[512,1024]{1,0:T(8,128)(2,1)} collective-permute-done((bf16[512,1024]{1,0:T(8,128)(2,1)}, bf16[512,1024]{1,0:T(8,128)(2,1)}, u32[]{:S(2)}, u32[]{:S(2)}) %collective-permute-start.42) | collective-permute-done | bytes 1048608 | tf_op jit(solution)/shard_map/ppermute | solution.py:27
  793.0 3.1 collective-permute-done.111
  (713 shorter events, 327.9 us)
Async XLA Ops:
  2.8 153.1 %collective-permute-start.1 = (bf16[44,256]{1,0:T(8,128)(2,1)}, bf16[44,256]{1,0:T(8,128)(2,1)}, u32[]{:S(2)}, u32[]{:S(2)}) collective-permute-start(bf16[44,256]{1,0:T(8,128)(2,1)} %get-tuple-element.281), channel_id=1, source_target_pairs={{0,1},{1,0},{2,3},{3,2},{4,5},{5,4},{6,7},{7,6},{8,9},{9,8},{10,11... | collective-permute-start | bytes 67592 | tf_op jit(solution)/shard_map/ppermute | solution.py:27
  5.9 150.1 %collective-permute-start.2 = (bf16[44,256]{1,0:T(8,128)(2,1)}, bf16[44,256]{1,0:T(8,128)(2,1)}, u32[]{:S(2)}, u32[]{:S(2)}) collective-permute-start(bf16[44,256]{1,0:T(8,128)(2,1)} %get-tuple-element.281), channel_id=1, source_target_pairs={{0,2},{1,3},{2,0},{3,1},{4,6},{5,7},{6,4},{7,5},{8,10},{9,11},{10,... | collective-permute-start | bytes 67592 | tf_op jit(solution)/shard_map/ppermute | solution.py:27
  8.4 147.5 %collective-permute-start.3 = (bf16[44,256]{1,0:T(8,128)(2,1)}, bf16[44,256]{1,0:T(8,128)(2,1)}, u32[]{:S(2)}, u32[]{:S(2)}) collective-permute-start(bf16[44,256]{1,0:T(8,128)(2,1)} %get-tuple-element.281), channel_id=1, source_target_pairs={{0,3},{1,2},{2,1},{3,0},{4,7},{5,6},{6,5},{7,4},{8,11},{9,10},{10,... | collective-permute-start | bytes 67592 | tf_op jit(solution)/shard_map/ppermute | solution.py:27
  9.8 148.2 %collective-permute-start = (bf16[16,1024]{1,0:T(8,128)(2,1)}, bf16[16,1024]{1,0:T(8,128)(2,1)}, u32[]{:S(2)}, u32[]{:S(2)}) collective-permute-start(bf16[16,1024]{1,0:T(8,128)(2,1)} %dynamic-slice_bitcast_fusion.2), channel_id=1, source_target_pairs={{0,4},{4,8},{8,12},{12,16},{16,20},{20,24},{24,28},{1,5},{5,9},{9,... | collective-permute-start | bytes 98312 | tf_op jit(solution)/shard_map/ppermute | solution.py:1053
  208.8 139.4 %collective-permute-start.51 = (bf16[512,512]{1,0:T(8,128)(2,1)}, bf16[512,512]{1,0:T(8,128)(2,1)S(1)}, u32[]{:S(2)}, u32[]{:S(2)}) collective-permute-start(bf16[512,512]{1,0:T(8,128)(2,1)} %pad_maximum_fusion.6), channel_id=1, source_target_pairs={{0,4},{4,0},{8,12},{12,8},{16,20},{20,16},{24,28},{28,24},{1,5},{5... | collective-permute-start | bytes 1572872 | tf_op jit(solution)/shard_map/ppermute | solution.py:23
  304.3 46.9 %collective-permute-start.30 = (bf16[2,2,128,128]{3,2,1,0:T(8,128)(2,1)}, bf16[2,2,128,128]{3,2,1,0:T(8,128)(2,1)}, u32[]{:S(2)}, u32[]{:S(2)}) collective-permute-start(bf16[2,2,128,128]{3,2,1,0:T(8,128)(2,1)} %get-tuple-element.268), channel_id=1, source_target_pairs={{0,16},{4,20},{8,24},{12,28},{16,0},{20,4},{24,8},{28,12},{1,17},{... | collective-permute-start | bytes 393224 | tf_op jit(solution)/shard_map/ppermute | solution.py:23
  305.3 46.1 %collective-permute-start.26 = (bf16[2,2,128,128]{3,2,1,0:T(8,128)(2,1)}, bf16[2,2,128,128]{3,2,1,0:T(8,128)(2,1)}, u32[]{:S(2)}, u32[]{:S(2)}) collective-permute-start(bf16[2,2,128,128]{3,2,1,0:T(8,128)(2,1)} %get-tuple-element.268), channel_id=1, source_target_pairs={{0,8},{4,12},{8,0},{12,4},{16,24},{20,28},{24,16},{28,20},{1,9},{5... | collective-permute-start | bytes 393224 | tf_op jit(solution)/shard_map/ppermute | solution.py:23
  318.7 30.7 %collective-permute-start.55 = (bf16[512,256]{1,0:T(8,128)(2,1)}, bf16[512,256]{1,0:T(8,128)(2,1)}, u32[]{:S(2)}, u32[]{:S(2)}) collective-permute-start(bf16[512,256]{1,0:T(8,128)(2,1)} %get-tuple-element.242), channel_id=1, source_target_pairs={{0,4},{4,0},{8,12},{12,8},{16,20},{20,16},{24,28},{28,24},{1,5},{5... | collective-permute-start | bytes 786440 | tf_op jit(solution)/shard_map/ppermute | solution.py:23
  318.7 30.7 %collective-permute-start.25 = (bf16[2,2,128,128]{3,2,1,0:T(8,128)(2,1)}, bf16[2,2,128,128]{3,2,1,0:T(8,128)(2,1)}, u32[]{:S(2)}, u32[]{:S(2)}) collective-permute-start(bf16[2,2,128,128]{3,2,1,0:T(8,128)(2,1)} %get-tuple-element.267), channel_id=1, source_target_pairs={{0,8},{4,12},{8,0},{12,4},{16,24},{20,28},{24,16},{28,20},{1,9},{5... | collective-permute-start | bytes 393224 | tf_op jit(solution)/shard_map/ppermute | solution.py:23
  363.0 195.3 %collective-permute-start.18 = (bf16[512,1024]{1,0:T(8,128)(2,1)}, bf16[512,1024]{1,0:T(8,128)(2,1)}, u32[]{:S(2)}, u32[]{:S(2)}) collective-permute-start(bf16[512,1024]{1,0:T(8,128)(2,1)} %get-tuple-element.117), channel_id=1, source_target_pairs={{0,1},{1,0},{2,3},{3,2},{4,5},{5,4},{6,7},{7,6},{8,9},{9,8},{10,11... | collective-permute-start | bytes 3145736 | tf_op jit(solution)/shard_map/ppermute | solution.py:27
  363.0 100.5 %collective-permute-start.91 = (bf16[512,704]{0,1:T(8,128)(2,1)}, bf16[512,704]{0,1:T(8,128)(2,1)}, u32[]{:S(2)}, u32[]{:S(2)}) collective-permute-start(bf16[512,704]{0,1:T(8,128)(2,1)} %copy.242), channel_id=1, source_target_pairs={{0,4},{4,0},{8,12},{12,8},{16,20},{20,16},{24,28},{28,24},{1,5},{5... | collective-permute-start | bytes 2162696 | tf_op jit(solution)/shard_map/ppermute | solution.py:23
  363.5 37.9 %collective-permute-start.63 = (bf16[512,256]{1,0:T(8,128)(2,1)S(1)}, bf16[512,256]{1,0:T(8,128)(2,1)S(1)}, u32[]{:S(2)}, u32[]{:S(2)}) collective-permute-start(bf16[512,256]{1,0:T(8,128)(2,1)S(1)} %copy-done.83), channel_id=1, source_target_pairs={{0,4},{4,0},{8,12},{12,8},{16,20},{20,16},{24,28},{28,24},{1,5},{5... | collective-permute-start | bytes 786440 | tf_op jit(solution)/shard_map/ppermute | solution.py:23
  405.6 34.8 %collective-permute-start.56 = (bf16[512,512]{1,0:T(8,128)(2,1)S(1)}, bf16[512,512]{1,0:T(8,128)(2,1)S(1)}, u32[]{:S(2)}, u32[]{:S(2)}) collective-permute-start(bf16[512,512]{1,0:T(8,128)(2,1)S(1)} %pad_maximum_fusion.8), channel_id=1, source_target_pairs={{0,4},{4,0},{8,12},{12,8},{16,20},{20,16},{24,28},{28,24},{1,5},{5... | collective-permute-start | bytes 1572872 | tf_op jit(solution)/shard_map/ppermute | solution.py:23
  407.8 32.4 %collective-permute-start.57 = (bf16[512,256]{1,0:T(8,128)(2,1)S(1)}, bf16[512,256]{1,0:T(8,128)(2,1)S(1)}, u32[]{:S(2)}, u32[]{:S(2)}) collective-permute-start(bf16[512,256]{1,0:T(8,128)(2,1)S(1)} %copy-done.82), channel_id=1, source_target_pairs={{0,4},{4,0},{8,12},{12,8},{16,20},{20,16},{24,28},{28,24},{1,5},{5... | collective-permute-start | bytes 786440 | tf_op jit(solution)/shard_map/ppermute | solution.py:23
  461.6 175.3 %collective-permute-start.20 = (bf16[512,1024]{1,0:T(8,128)(2,1)}, bf16[512,1024]{1,0:T(8,128)(2,1)}, u32[]{:S(2)}, u32[]{:S(2)}) collective-permute-start(bf16[512,1024]{1,0:T(8,128)(2,1)} %get-tuple-element.117), channel_id=1, source_target_pairs={{1,2},{2,1},{5,6},{6,5},{9,10},{10,9},{13,14},{14,13},{17,18},{18,... | collective-permute-start | bytes 3145736 | tf_op jit(solution)/shard_map/ppermute | solution.py:27
  493.5 33.9 %collective-permute-start.94 = (bf16[512,704]{0,1:T(8,128)(2,1)}, bf16[512,704]{0,1:T(8,128)(2,1)}, u32[]{:S(2)}, u32[]{:S(2)}) collective-permute-start(bf16[512,704]{0,1:T(8,128)(2,1)} %copy.246), channel_id=1, source_target_pairs={{0,4},{4,0},{8,12},{12,8},{16,20},{20,16},{24,28},{28,24},{1,5},{5... | collective-permute-start | bytes 2162696 | tf_op jit(solution)/shard_map/ppermute | solution.py:23
  503.1 112.0 %collective-permute-start.38 = (bf16[512,1024]{1,0:T(8,128)(2,1)}, bf16[512,1024]{1,0:T(8,128)(2,1)}, u32[]{:S(2)}, u32[]{:S(2)}) collective-permute-start(bf16[512,1024]{1,0:T(8,128)(2,1)} %get-tuple-element.128), channel_id=1, source_target_pairs={{0,1},{1,0},{2,3},{3,2},{4,5},{5,4},{6,7},{7,6},{8,9},{9,8},{10,11... | collective-permute-start | bytes 3145736 | tf_op jit(solution)/shard_map/ppermute | solution.py:27
  551.2 84.6 %collective-permute-start.92 = (bf16[3,2,128,704]{2,3,0,1:T(8,128)(2,1)S(1)}, bf16[3,2,128,704]{2,3,0,1:T(8,128)(2,1)S(1)}, u32[]{:S(2)}, u32[]{:S(2)}) collective-permute-start(bf16[3,2,128,704]{2,3,0,1:T(8,128)(2,1)S(1)} %pad_maximum_fusion.1), channel_id=1, source_target_pairs={{0,8},{4,12},{8,0},{12,4},{16,24},{20,28},{24,16},{28,20},{1,9},{5... | collective-permute-start | bytes 3244040 | tf_op jit(solution)/shard_map/ppermute | solution.py:23
  601.6 36.9 %collective-permute-start.102 = (bf16[3,2,128,704]{2,3,0,1:T(8,128)(2,1)S(1)}, bf16[3,2,128,704]{2,3,0,1:T(8,128)(2,1)S(1)}, u32[]{:S(2)}, u32[]{:S(2)}) collective-permute-start(bf16[3,2,128,704]{2,3,0,1:T(8,128)(2,1)S(1)} %pad_maximum_fusion.3), channel_id=1, source_target_pairs={{0,8},{4,12},{8,0},{12,4},{16,24},{20,28},{24,16},{28,20},{1,9},{5... | collective-permute-start | bytes 3244040 | tf_op jit(solution)/shard_map/ppermute | solution.py:23
  615.1 43.4 %collective-permute-start.107 = (bf16[3,2,128,704]{2,3,0,1:T(8,128)(2,1)S(1)}, bf16[3,2,128,704]{2,3,0,1:T(8,128)(2,1)S(1)}, u32[]{:S(2)}, u32[]{:S(2)}) collective-permute-start(bf16[3,2,128,704]{2,3,0,1:T(8,128)(2,1)S(1)} %pad_maximum_fusion.4), channel_id=1, source_target_pairs={{0,8},{4,12},{8,0},{12,4},{16,24},{20,28},{24,16},{28,20},{1,9},{5... | collective-permute-start | bytes 3244040 | tf_op jit(solution)/shard_map/ppermute | solution.py:23
  635.4 46.3 %collective-permute-start.97 = (bf16[3,2,128,704]{2,3,0,1:T(8,128)(2,1)S(1)}, bf16[3,2,128,704]{2,3,0,1:T(8,128)(2,1)S(1)}, u32[]{:S(2)}, u32[]{:S(2)}) collective-permute-start(bf16[3,2,128,704]{2,3,0,1:T(8,128)(2,1)S(1)} %pad_maximum_fusion.2), channel_id=1, source_target_pairs={{0,8},{4,12},{8,0},{12,4},{16,24},{20,28},{24,16},{28,20},{1,9},{5... | collective-permute-start | bytes 3244040 | tf_op jit(solution)/shard_map/ppermute | solution.py:23
  635.8 53.9 %collective-permute-start.40 = (bf16[512,1024]{1,0:T(8,128)(2,1)}, bf16[512,1024]{1,0:T(8,128)(2,1)S(1)}, u32[]{:S(2)}, u32[]{:S(2)}) collective-permute-start(bf16[512,1024]{1,0:T(8,128)(2,1)} %get-tuple-element.128), channel_id=1, source_target_pairs={{1,2},{2,1},{5,6},{6,5},{9,10},{10,9},{13,14},{14,13},{17,18},{18,... | collective-permute-start | bytes 3145736 | tf_op jit(solution)/shard_map/ppermute | solution.py:27
  636.8 63.4 %collective-permute-start.19 = (bf16[512,1024]{1,0:T(8,128)(2,1)}, bf16[512,1024]{1,0:T(8,128)(2,1)}, u32[]{:S(2)}, u32[]{:S(2)}) collective-permute-start(bf16[512,1024]{1,0:T(8,128)(2,1)} %collective-permute-done.18), channel_id=1, source_target_pairs={{1,2},{2,1},{5,6},{6,5},{9,10},{10,9},{13,14},{14,13},{17,18},{18,... | collective-permute-start | bytes 3145736 | tf_op jit(solution)/shard_map/ppermute | solution.py:27
  638.5 62.1 %collective-permute-start.21 = (bf16[512,1024]{1,0:T(8,128)(2,1)}, bf16[512,1024]{1,0:T(8,128)(2,1)S(1)}, u32[]{:S(2)}, u32[]{:S(2)}) collective-permute-start(bf16[512,1024]{1,0:T(8,128)(2,1)} %collective-permute-done.20), channel_id=1, source_target_pairs={{2,3},{1,0},{6,7},{5,4},{10,11},{9,8},{14,15},{13,12},{18,19},{17,... | collective-permute-start | bytes 3145736 | tf_op jit(solution)/shard_map/ppermute | solution.py:27
  698.9 37.0 %collective-permute-start.41 = (bf16[512,1024]{1,0:T(8,128)(2,1)S(1)}, bf16[512,1024]{1,0:T(8,128)(2,1)S(1)}, u32[]{:S(2)}, u32[]{:S(2)}) collective-permute-start(bf16[512,1024]{1,0:T(8,128)(2,1)S(1)} %collective-permute-done.40), channel_id=1, source_target_pairs={{2,3},{1,0},{6,7},{5,4},{10,11},{9,8},{14,15},{13,12},{18,19},{17,... | collective-permute-start | bytes 3145736 | tf_op jit(solution)/shard_map/ppermute | solution.py:27
  709.0 30.3 %collective-permute-start.59 = (bf16[5,128,256]{2,1,0:T(8,128)(2,1)S(1)}, bf16[5,128,256]{2,1,0:T(8,128)(2,1)S(1)}, u32[]{:S(2)}, u32[]{:S(2)}) collective-permute-start(bf16[5,128,256]{2,1,0:T(8,128)(2,1)S(1)} %slice_bitcast_fusion.29), channel_id=1, source_target_pairs={{0,8},{4,12},{8,0},{12,4},{16,24},{20,28},{24,16},{28,20},{1,9},{5... | collective-permute-start | bytes 983048 | tf_op jit(solution)/shard_map/ppermute | solution.py:23
  710.6 29.6 %collective-permute-start.85 = (bf16[5,128,256]{2,1,0:T(8,128)(2,1)S(1)}, bf16[5,128,256]{2,1,0:T(8,128)(2,1)S(1)}, u32[]{:S(2)}, u32[]{:S(2)}) collective-permute-start(bf16[5,128,256]{2,1,0:T(8,128)(2,1)S(1)} %add_convert_fusion.11), channel_id=1, source_target_pairs={{1,2},{2,1},{5,6},{6,5},{9,10},{10,9},{13,14},{14,13},{17,18},{18,... | collective-permute-start | bytes 983048 | tf_op jit(solution)/shard_map/ppermute | solution.py:27
  711.3 30.2 %collective-permute-start.83 = (bf16[5,128,256]{2,1,0:T(8,128)(2,1)S(1)}, bf16[5,128,256]{2,1,0:T(8,128)(2,1)S(1)}, u32[]{:S(2)}, u32[]{:S(2)}) collective-permute-start(bf16[5,128,256]{2,1,0:T(8,128)(2,1)S(1)} %get-tuple-element.175), channel_id=1, source_target_pairs={{2,3},{1,0},{6,7},{5,4},{10,11},{9,8},{14,15},{13,12},{18,19},{17,... | collective-permute-start | bytes 983048 | tf_op jit(solution)/shard_map/ppermute | solution.py:27
  741.5 49.0 %collective-permute-start.42 = (bf16[512,1024]{1,0:T(8,128)(2,1)}, bf16[512,1024]{1,0:T(8,128)(2,1)}, u32[]{:S(2)}, u32[]{:S(2)}) collective-permute-start(bf16[512,1024]{1,0:T(8,128)(2,1)} %collective-permute-done.39), channel_id=1, source_target_pairs={{2,3},{1,0},{6,7},{5,4},{10,11},{9,8},{14,15},{13,12},{18,19},{17,... | collective-permute-start | bytes 3145736 | tf_op jit(solution)/shard_map/ppermute | solution.py:27
  748.8 44.3 %collective-permute-start.93 = (bf16[3,128,704]{1,2,0:T(8,128)(2,1)}, bf16[3,128,704]{1,2,0:T(8,128)(2,1)S(1)}, u32[]{:S(2)}, u32[]{:S(2)}) collective-permute-start(bf16[3,128,704]{1,2,0:T(8,128)(2,1)} %slice_bitcast_fusion.18), channel_id=1, source_target_pairs={{0,16},{4,20},{8,24},{12,28},{16,0},{20,4},{24,8},{28,12},{1,17},{... | collective-permute-start | bytes 1622024 | tf_op jit(solution)/shard_map/ppermute | solution.py:23
  751.9 41.1 %collective-permute-start.113 = (bf16[3,128,704]{1,2,0:T(8,128)(2,1)S(1)}, bf16[3,128,704]{1,2,0:T(8,128)(2,1)S(1)}, u32[]{:S(2)}, u32[]{:S(2)}) collective-permute-start(bf16[3,128,704]{1,2,0:T(8,128)(2,1)S(1)} %add_convert_fusion.8), channel_id=1, source_target_pairs={{1,2},{2,1},{5,6},{6,5},{9,10},{10,9},{13,14},{14,13},{17,18},{18,... | collective-permute-start | bytes 1622024 | tf_op jit(solution)/shard_map/ppermute | solution.py:27
  754.1 42.0 %collective-permute-start.111 = (bf16[3,128,704]{1,2,0:T(8,128)(2,1)S(1)}, bf16[3,128,704]{1,2,0:T(8,128)(2,1)S(1)}, u32[]{:S(2)}, u32[]{:S(2)}) collective-permute-start(bf16[3,128,704]{1,2,0:T(8,128)(2,1)S(1)} %get-tuple-element.171), channel_id=1, source_target_pairs={{2,3},{1,0},{6,7},{5,4},{10,11},{9,8},{14,15},{13,12},{18,19},{17,... | collective-permute-start | bytes 1622024 | tf_op jit(solution)/shard_map/ppermute | solution.py:27
  (196 other events, 1798.4 us)
